TPU v7x, 32 devices: a whole 2x2x4 slice. The times are simulated.
32 devices in a mesh: nodes: 8 (over y, x, core), cols: 4 (over z).
Axes of the slice: x: 2, y: 2, z: 4, core: 2. Of those that a mesh axis runs over, the one named last changes fastest.
Arguments:
- prior: float32 [65536, 128], P(('nodes', 'cols')), may hold values from -18 to 18
- queries: int32 [128], replicated, may hold values from 0 to 65535
- tile_rows: int32 [2048], P(('nodes', 'cols')), may hold values from -1 to 511, as said below
- tile_cols: int32 [2048], P(('nodes', 'cols')), may hold values from -1 to 511
- tile_ids: int32 [2048, 8, 128], P(('nodes', 'cols')), may hold values from 0 to 127
- tile_weights: float32 [2048, 8, 128], P(('nodes', 'cols')), may hold values from 0.1 to 1
Outputs:
- solution: float32 [65536, 128], P(('nodes', 'cols'))
- residual: float32 [65536, 128], P(('nodes', 'cols'))
Inputs may be any that keep to these rules, and one draw needn't show every extreme that they name: Tiles come in 8 node groups of 64 consecutive row blocks; the slots of the devices of group g hold only tiles with row blocks in group g. A live tile's column block is at most 4 blocks from its row block; every block's diagonal tile is present; no block pair appears twice. An empty slot has -1 in both tile_rows and tile_cols.
All inputs are finite; a program needn't handle non-finite values.
Results may differ from a plain program's by a relative error of at most 0.0017.
Values sent between devices are 32-bit elements; how exact they have to be, the bound alone decides.
A program may use at most 128 MiB of HBM per device.

v0:
```python
import jax
import jax.numpy as jnp
from jax import lax
from jax.sharding import PartitionSpec as P

TB = 128
KT = 8
BAND = 4
ITERS = 3


HIGH = lax.Precision.HIGHEST
ALPHA = 0.9
BOOST = 4.0


def shifted(block, axis, distance):
    devices = range(lax.axis_size(axis))
    route = [(i - distance, i) for i in devices if i - distance in devices]
    return lax.ppermute(block, axis, route)


def with_halo(cells, sides, width):
    for axis, dim in sides:
        count = lax.axis_size(axis)
        ends = count - 1
        head = lax.slice_in_dim(cells, 0, width, axis=dim)
        tail = lax.slice_in_dim(cells, cells.shape[dim] - width, cells.shape[dim], axis=dim)
        cells = jnp.concatenate(
            [
                lax.ppermute(tail, axis, [(i, (i + 1) % count) for i in range(ends)]),
                cells,
                lax.ppermute(head, axis, [((i + 1) % count, i) for i in range(ends)]),
            ],
            axis=dim,
        )
    return cells


def dense_tiles(tile_ids, tile_weights):
    columns = jnp.arange(TB, dtype=jnp.int32)
    total_sum = jnp.zeros((tile_ids.shape[0], TB, TB), jnp.float32)
    for slot_index in range(KT):
        matched = (tile_ids[:, slot_index, :, None] == columns[None, None, :]).astype(jnp.float32)
        total_sum = total_sum + tile_weights[:, slot_index, :, None] * matched
    return total_sum


def inner_gram(left_vec, right_vec):
    return jnp.einsum("nq,np->qp", left_vec, right_vec, precision=HIGH)


def solve_gram(matrix, right_side):
    return jax.scipy.linalg.cho_solve((jnp.linalg.cholesky(matrix), True), right_side)


def residual_square(residual):
    return lax.psum(inner_gram(residual, residual), ("nodes", "cols"))


def hot_table(spots, where_at):
    return (spots[:, None] == where_at[None, :]).astype(jnp.float32)


def tile_terms(dense_tile, rows_at, cols_at, pieces, spots):
    ext_count = pieces.shape[0]
    row_safe = jnp.clip(rows_at, 0, ext_count - 1)
    col_safe = jnp.clip(cols_at, 0, ext_count - 1)
    backward = jnp.einsum("tjr,tjq->trq", dense_tile, pieces[row_safe], precision=HIGH)
    result = jnp.einsum("st,trq->srq", hot_table(spots, cols_at), backward, precision=HIGH)
    forward = jnp.einsum("trj,tjq->trq", dense_tile, pieces[col_safe], precision=HIGH)
    result = result + jnp.einsum("st,trq->srq", hot_table(spots, rows_at), forward, precision=HIGH)
    return result


def body(prior, queries, tile_rows, tile_cols, tile_ids, tile_weights):
    rows_dev, query_width = prior.shape
    col_count = lax.axis_size("cols")
    node_index = lax.axis_index("nodes")
    member = lax.axis_index("cols")
    group_rows = rows_dev * col_count
    blocks = group_rows // TB
    ext_blocks = blocks + 2 * BAND
    first_block = node_index * blocks
    places = jnp.arange(ext_blocks, dtype=jnp.int32)
    pair_float = jnp.stack([tile_rows, tile_cols], axis=1).astype(jnp.float32)
    ids_float = tile_ids.astype(jnp.float32)
    pair_int = pair_float.astype(jnp.int32)
    live_slot = pair_int[:, 0] >= 0
    rows_at = jnp.where(live_slot, pair_int[:, 0] - first_block + BAND, -1)
    cols_at = jnp.where(live_slot, pair_int[:, 1] - first_block + BAND, -1)
    dense_tile = (
        dense_tiles(ids_float.astype(jnp.int32), tile_weights)
        * live_slot.astype(jnp.float32)[:, None, None]
    )
    local_degree = jnp.dot(
        hot_table(places, rows_at), jnp.sum(dense_tile, axis=2), precision=HIGH
    ) + jnp.dot(hot_table(places, cols_at), jnp.sum(dense_tile, axis=1), precision=HIGH)
    group_degree = lax.psum(local_degree, "cols")
    degree_mid = group_degree[BAND : BAND + blocks]
    degree_rims = []
    for toward, outgoing in ((1, group_degree[BAND + blocks :]), (-1, group_degree[:BAND])):
        degree_rims.append(shifted(outgoing, "nodes", toward))
    degree_mid = degree_mid.at[:BAND].add(degree_rims[0]).at[blocks - BAND :].add(degree_rims[1])
    degree = lax.dynamic_slice_in_dim(degree_mid.reshape(-1), member * rows_dev, rows_dev)
    inv_root = lax.rsqrt(degree)[:, None]
    global_rows = (node_index * col_count + member) * rows_dev + jnp.arange(
        rows_dev, dtype=jnp.int32
    )
    target = prior + BOOST * (global_rows[:, None] == queries[None, :]).astype(jnp.float32)
    solution = jnp.zeros_like(target)
    residual = target
    direction = target
    gram = residual_square(residual)
    for iteration in range(ITERS):
        scaled = inv_root * direction
        group_vec = lax.all_gather(scaled, "cols", axis=0, tiled=True)
        widened = with_halo(group_vec, (("nodes", 0),), BAND * TB)
        pieces = widened.reshape(ext_blocks, TB, query_width)
        partial_sum = tile_terms(dense_tile, rows_at, cols_at, pieces, places)
        middle = partial_sum[BAND : BAND + blocks]
        arrived_rows = []
        for fold_toward, fold_outgoing in (
            (1, partial_sum[BAND + blocks :]),
            (-1, partial_sum[:BAND]),
        ):
            arrived_rows.append(shifted(fold_outgoing, "nodes", fold_toward))
        graph_middle = (
            middle.at[:BAND].add(arrived_rows[0]).at[blocks - BAND :].add(arrived_rows[1])
        )
        summed = lax.psum_scatter(
            graph_middle.reshape(group_rows, query_width), "cols", scatter_dimension=0, tiled=True
        )
        image_vec = direction - ALPHA * inv_root * summed
        curvature, cross_gram, square = lax.psum(
            (
                inner_gram(direction, image_vec),
                inner_gram(image_vec, residual),
                inner_gram(image_vec, image_vec),
            ),
            ("nodes", "cols"),
        )
        step_mat = solve_gram(curvature, gram)
        solution = solution + jnp.dot(direction, step_mat, precision=HIGH)
        residual = residual - jnp.dot(image_vec, step_mat, precision=HIGH)
        carried = jnp.dot(cross_gram.T, step_mat, precision=HIGH)
        gram_new = (
            gram
            - carried
            - carried.T
            + jnp.dot(step_mat.T, jnp.dot(square, step_mat, precision=HIGH), precision=HIGH)
        )
        ratio_mat = solve_gram(gram, gram_new)
        direction = residual + jnp.dot(direction, ratio_mat, precision=HIGH)
        gram = gram_new
    return (solution, residual)


def solution(mesh):
    in_specs = (
        P(("nodes", "cols"), None),
        P(),
        P(("nodes", "cols")),
        P(("nodes", "cols")),
        P(("nodes", "cols"), None, None),
        P(("nodes", "cols"), None, None),
    )
    out_specs = (P(("nodes", "cols"), None), P(("nodes", "cols"), None))
    return jax.shard_map(body, mesh=mesh, in_specs=in_specs, out_specs=out_specs, check_vma=False)
```

profile of v0, /device:TPU:0, one launch (start us, length us, event | category | flops | bytes accessed | tf_op | source)
XLA Modules:
  0.0 1446.9 jit_solution(17337139558166330666)
XLA Ops:
  11.6 20.2 %fusion.97 = (f32[64,128]{1,0:T(8,128)S(1)}, f32[64,128]{1,0:T(8,128)S(1)}) fusion(f32[64]{0:T(128)S(1)} %convert_bitcast_fusion, f32[64,128]{1,0:T(8,128)S(1)} %bitcast.264, s32[64,128]{1,0:T(8,128)S(1)} %bitcast.173, f32[64,128]{1,0:T(8,128)S(1)} %bitcast.271, s32[64,128]{1,0:T(8,128)S(1)} %bitcast.180, f32[64,128]{1,0:T(8,128)S(1)} %bitcast.229, ...), kind=kLoop, calls=%fused_computation.167 | loop fusion | flops 27246592 | bytes 590080 | tf_op jit(solution)/shard_map/reduce_sum | solution.py:98
  32.5 21.2 %psum.63 = f32[72,128]{1,0:T(8,128)S(1)} all-reduce(f32[72,128]{1,0:T(8,128)S(1)} %convolution_add_fusion.6), channel_id=1, replica_groups=mesh['nodes'=8,'cols'=4] {'cols'}, use_global_device_ids=true, to_apply=%region_2.3 | all-reduce | flops 9216 | bytes 73728 | tf_op jit(solution)/shard_map/psum | solution.py:99
  62.4 81.0 %all-gather.4.cloned.1.call-done = f32[8192,128]{1,0:T(8,128)} async-done(((f32[2048,128]{1,0:T(8,128)}), f32[8192,128]{1,0:T(8,128)}) %all-gather.4.cloned.1.call-update) | async-done | bytes 4194320 | tf_op jit(solution)/shard_map/all_gather | solution.py:117
  151.0 4.9 pad_maximum_fusion
  155.9 5.2 gather_fusion
  161.1 34.1 %fusion.96 = f32[64,128,128]{2,1,0:T(8,128)} fusion(f32[64,128,128]{2,1,0:T(8,128)} %gather_fusion, f32[64]{0:T(128)S(1)} %convert_bitcast_fusion, f32[64,128]{1,0:T(8,128)S(1)} %bitcast.265, s32[64,128]{1,0:T(8,128)S(1)} %bitcast.174, f32[64,128]{1,0:T(8,128)S(1)} %bitcast.272, s32[64,128]{1,0:T(8,128)S(1)} %bitcast.181, f32[64,128]{1,0:T(8,128)S(1)} %bitcast.230, ...), kind=kOutput, calls=%fused_computation.166 | convolution fusion | flops 1635778560 | bytes 8913152 | tf_op jit(solution)/shard_map/tjr,tjq->trq/dot_general | solution.py:69
  195.3 5.2 gather_fusion.1
  200.6 35.3 %fusion.95 = f32[64,128,128]{2,1,0:T(8,128)S(1)} fusion(f32[64,128,128]{2,1,0:T(8,128)} %gather_fusion.1, f32[64]{0:T(128)S(1)} %convert_bitcast_fusion, f32[64,128]{1,0:T(8,128)S(1)} %bitcast.266, s32[64,128]{1,0:T(8,128)S(1)} %bitcast.175, f32[64,128]{1,0:T(8,128)S(1)} %bitcast.273, s32[64,128]{1,0:T(8,128)S(1)} %bitcast.182, ...), kind=kOutput, calls=%fused_computation.165 | convolution fusion | flops 1635778560 | bytes 8913152 | tf_op jit(solution)/shard_map/trj,tjq->trq/dot_general | solution.py:71
  236.0 5.0 fusion.8
  241.0 5.2 fusion.12
  246.3 6.7 collective-permute-start.4
  256.6 4.4 copy.42
  265.3 75.9 %reduce-scatter.4.cloned.1.call-done = f32[2048,128]{1,0:T(8,128)} async-done(((f32[8192,128]{1,0:T(8,128)}), f32[2048,128]{1,0:T(8,128)}) %reduce-scatter.4.cloned.1.call-update) | async-done | bytes 1048592 | tf_op jit(solution)/shard_map/reduce_scatter | solution.py:131
  341.2 4.7 fusion.23
  345.9 5.2 fusion.22
  354.6 126.5 %all-reduce.10.cloned.1.call-done = (f32[128,128]{0,1:T(8,128)}, f32[128,128]{0,1:T(8,128)}, f32[128,128]{1,0:T(8,128)}, f32[128,128]{1,0:T(8,128)}) async-done(((f32[128,128]{0,1:T(8,128)}, f32[128,128]{0,1:T(8,128)}, f32[128,128]{1,0:T(8,128)}, f32[128,128]{1,0:T(8,128)}), (f32[128,128]{0,1:T(8,128)}, f32[128,128]{0,1:T(8,128)}, f32[128,128]{1,0:T(8,128)}, ...) | async-done | bytes 262160 | tf_op jit(solution)/shard_map/psum | solution.py:58
  482.9 11.7 cholesky.89
  495.9 9.8 custom-call.11
  511.2 11.7 cholesky.100
  524.2 10.2 custom-call.12
  540.5 79.9 %all-gather.6.cloned.1.call-done = f32[8192,128]{1,0:T(8,128)} async-done(((f32[2048,128]{1,0:T(8,128)}), f32[8192,128]{1,0:T(8,128)}) %all-gather.6.cloned.1.call-update) | async-done | bytes 4194320 | tf_op jit(solution)/shard_map/all_gather | solution.py:117
  627.9 4.9 pad_maximum_fusion.1
  632.8 5.2 gather_fusion.2
  638.2 5.3 gather_fusion.3
  643.6 41.1 %fusion.94 = f32[64,128,128]{2,1,0:T(8,128)S(1)} fusion(f32[64,128,128]{2,1,0:T(8,128)} %gather_fusion.2, f32[64]{0:T(128)S(1)} %convert_bitcast_fusion, f32[64,128]{1,0:T(8,128)S(1)} %bitcast.268, s32[64,128]{1,0:T(8,128)S(1)} %bitcast.176, f32[64,128]{1,0:T(8,128)S(1)} %bitcast.275, s32[64,128]{1,0:T(8,128)S(1)} %bitcast.183, ...), kind=kOutput, calls=%fused_computation.164 | convolution fusion | flops 1635778560 | bytes 8913152 | tf_op jit(solution)/shard_map/tjr,tjq->trq/dot_general | solution.py:69
  684.7 33.3 %fusion.93 = f32[64,128,128]{2,1,0:T(8,128)S(1)} fusion(f32[64,128,128]{2,1,0:T(8,128)S(1)} %copy-done.5, f32[64]{0:T(128)S(1)} %convert_bitcast_fusion, f32[64,128]{1,0:T(8,128)S(1)} %bitcast.269, s32[64,128]{1,0:T(8,128)S(1)} %bitcast.177, f32[64,128]{1,0:T(8,128)S(1)} %bitcast.276, s32[64,128]{1,0:T(8,128)S(1)} %bitcast.184, ...), kind=kOutput, calls=%fused_computation.163 | convolution fusion | flops 1635778560 | bytes 8913152 | tf_op jit(solution)/shard_map/trj,tjq->trq/dot_general | solution.py:71
  718.0 5.0 fusion.4
  723.0 5.2 fusion.15
  728.3 6.7 collective-permute-start.8
  743.2 11.7 cholesky.122
  755.6 67.8 %reduce-scatter.6.cloned.1.call-done = f32[2048,128]{1,0:T(8,128)} async-done(((f32[8192,128]{1,0:T(8,128)}), f32[2048,128]{1,0:T(8,128)}) %reduce-scatter.6.cloned.1.call-update) | async-done | bytes 1048592 | tf_op jit(solution)/shard_map/reduce_scatter | solution.py:131
  834.6 9.8 custom-call.14
  844.4 114.0 %all-reduce.8.cloned.1.call-done = (f32[128,128]{0,1:T(8,128)}, f32[128,128]{1,0:T(8,128)}, f32[128,128]{1,0:T(8,128)}) async-done(((f32[128,128]{0,1:T(8,128)}, f32[128,128]{1,0:T(8,128)}, f32[128,128]{1,0:T(8,128)}), (f32[128,128]{0,1:T(8,128)}, f32[128,128]{1,0:T(8,128)}, f32[128,128]{1,0:T(8,128)})) %all-reduce.8.cloned.1.call-update) | async-done | bytes 196624 | tf_op jit(solution)/shard_map/psum | solution.py:135
  960.1 11.7 cholesky.111
  973.9 10.6 custom-call.13
  994.6 81.8 %all-gather.8.cloned.1.call-done = f32[8192,128]{1,0:T(8,128)} async-done(((f32[2048,128]{1,0:T(8,128)}), f32[8192,128]{1,0:T(8,128)}) %all-gather.8.cloned.1.call-update) | async-done | bytes 4194320 | tf_op jit(solution)/shard_map/all_gather | solution.py:117
  1083.9 4.9 pad_maximum_fusion.2
  1088.8 5.2 gather_fusion.4
  1094.1 5.2 gather_fusion.5
  1099.4 46.5 %fusion.92 = f32[64,128,128]{2,1,0:T(8,128)S(1)} fusion(f32[64,128,128]{2,1,0:T(8,128)} %gather_fusion.4, f32[64]{0:T(128)S(1)} %convert_bitcast_fusion, f32[64,128]{1,0:T(8,128)} %bitcast.267, s32[64,128]{1,0:T(8,128)S(1)} %bitcast.178, f32[64,128]{1,0:T(8,128)} %bitcast.274, s32[64,128]{1,0:T(8,128)S(1)} %bitcast.185, f32[64,128]{1,0:T(8,128)} %bitcast.232, ...), kind=kOutput, calls=%fused_computation.162 | convolution fusion | flops 1635778560 | bytes 8913152 | tf_op jit(solution)/shard_map/tjr,tjq->trq/dot_general | solution.py:69
  1146.1 33.3 %fusion.91 = f32[64,128,128]{2,1,0:T(8,128)S(1)} fusion(f32[64,128,128]{2,1,0:T(8,128)S(1)} %copy-done.4, f32[64]{0:T(128)S(1)} %convert_bitcast_fusion, f32[64,128]{1,0:T(8,128)S(1)} %bitcast.270, s32[64,128]{1,0:T(8,128)S(1)} %bitcast.179, f32[64,128]{1,0:T(8,128)S(1)} %bitcast.277, s32[64,128]{1,0:T(8,128)S(1)} %bitcast.186, ...), kind=kOutput, calls=%fused_computation.161 | convolution fusion | flops 1635778560 | bytes 8913152 | tf_op jit(solution)/shard_map/trj,tjq->trq/dot_general | solution.py:71
  1179.4 5.0 fusion
  1184.4 5.2 fusion.18
  1189.7 6.7 collective-permute-start.12
  1206.6 78.0 %reduce-scatter.8.cloned.1.call-done = f32[2048,128]{1,0:T(8,128)} async-done(((f32[8192,128]{1,0:T(8,128)}), f32[2048,128]{1,0:T(8,128)}) %reduce-scatter.8.cloned.1.call-update) | async-done | bytes 1048592 | tf_op jit(solution)/shard_map/reduce_scatter | solution.py:131
  1291.9 117.9 %all-reduce.6.cloned.1.call-done = f32[128,128]{0,1:T(8,128)} async-done(((f32[128,128]{0,1:T(8,128)}), f32[128,128]{0,1:T(8,128)}) %all-reduce.6.cloned.1.call-update) | async-done | bytes 65552 | tf_op jit(solution)/shard_map/psum | solution.py:135
  1411.6 11.7 cholesky.133
  1424.7 9.8 custom-call.15
  (238 shorter events, 123.6 us)
Async XLA Ops:
  7.2 136.3 %all-gather.4.cloned.1.call-start = ((), (), s32[]{:S(2)}) async-start(), calls=%async_computation.3 | async-start | bytes 5242880 | tf_op jit(solution)/shard_map/all_gather | solution.py:117
  8.4 192.1 %copy-start.12 = (s32[64,1,128]{2,1,0:T(1,128)}, s32[64,1,128]{2,1,0:T(1,128)S(1)}, u32[]{:S(2)}) copy-start(s32[64,1,128]{2,1,0:T(1,128)S(1)} %get-tuple-element.130) | copy-start | bytes 98308
  8.4 192.1 %copy-start.15 = (s32[64,1,128]{2,1,0:T(1,128)}, s32[64,1,128]{2,1,0:T(1,128)S(1)}, u32[]{:S(2)}) copy-start(s32[64,1,128]{2,1,0:T(1,128)S(1)} %get-tuple-element.131) | copy-start | bytes 98308
  8.4 192.1 %copy-start.18 = (s32[64,1,128]{2,1,0:T(1,128)}, s32[64,1,128]{2,1,0:T(1,128)S(1)}, u32[]{:S(2)}) copy-start(s32[64,1,128]{2,1,0:T(1,128)S(1)} %get-tuple-element.132) | copy-start | bytes 98308
  8.4 192.1 %copy-start.21 = (s32[64,1,128]{2,1,0:T(1,128)}, s32[64,1,128]{2,1,0:T(1,128)S(1)}, u32[]{:S(2)}) copy-start(s32[64,1,128]{2,1,0:T(1,128)S(1)} %get-tuple-element.133) | copy-start | bytes 98308
  8.4 192.1 %copy-start.24 = (s32[64,1,128]{2,1,0:T(1,128)}, s32[64,1,128]{2,1,0:T(1,128)S(1)}, u32[]{:S(2)}) copy-start(s32[64,1,128]{2,1,0:T(1,128)S(1)} %get-tuple-element.134) | copy-start | bytes 98308
  8.4 676.2 %copy-start.8 = (s32[64,1,128]{2,1,0:T(1,128)}, s32[64,1,128]{2,1,0:T(1,128)S(1)}, u32[]{:S(2)}) copy-start(s32[64,1,128]{2,1,0:T(1,128)S(1)} %get-tuple-element.128) | copy-start | bytes 98308
  8.4 676.2 %copy-start.10 = (s32[64,1,128]{2,1,0:T(1,128)}, s32[64,1,128]{2,1,0:T(1,128)S(1)}, u32[]{:S(2)}) copy-start(s32[64,1,128]{2,1,0:T(1,128)S(1)} %get-tuple-element.129) | copy-start | bytes 98308
  10.8 189.8 %copy-start.27 = (f32[64,1,128]{2,1,0:T(1,128)}, f32[64,1,128]{2,1,0:T(1,128)S(1)}, u32[]{:S(2)}) copy-start(f32[64,1,128]{2,1,0:T(1,128)S(1)} %get-tuple-element.135) | copy-start | bytes 98308
  10.8 189.8 %copy-start.30 = (f32[64,1,128]{2,1,0:T(1,128)}, f32[64,1,128]{2,1,0:T(1,128)S(1)}, u32[]{:S(2)}) copy-start(f32[64,1,128]{2,1,0:T(1,128)S(1)} %get-tuple-element.136) | copy-start | bytes 98308
  10.8 189.8 %copy-start.33 = (f32[64,1,128]{2,1,0:T(1,128)}, f32[64,1,128]{2,1,0:T(1,128)S(1)}, u32[]{:S(2)}) copy-start(f32[64,1,128]{2,1,0:T(1,128)S(1)} %get-tuple-element.137) | copy-start | bytes 98308
  10.8 189.8 %copy-start.36 = (f32[64,1,128]{2,1,0:T(1,128)}, f32[64,1,128]{2,1,0:T(1,128)S(1)}, u32[]{:S(2)}) copy-start(f32[64,1,128]{2,1,0:T(1,128)S(1)} %get-tuple-element.138) | copy-start | bytes 98308
  10.8 189.8 %copy-start.39 = (f32[64,1,128]{2,1,0:T(1,128)}, f32[64,1,128]{2,1,0:T(1,128)S(1)}, u32[]{:S(2)}) copy-start(f32[64,1,128]{2,1,0:T(1,128)S(1)} %get-tuple-element.139) | copy-start | bytes 98308
  10.9 189.8 %copy-start.42 = (f32[64,1,128]{2,1,0:T(1,128)}, f32[64,1,128]{2,1,0:T(1,128)S(1)}, u32[]{:S(2)}) copy-start(f32[64,1,128]{2,1,0:T(1,128)S(1)} %get-tuple-element.140) | copy-start | bytes 98308
  10.9 189.8 %copy-start.45 = (f32[64,1,128]{2,1,0:T(1,128)}, f32[64,1,128]{2,1,0:T(1,128)S(1)}, u32[]{:S(2)}) copy-start(f32[64,1,128]{2,1,0:T(1,128)S(1)} %get-tuple-element.141) | copy-start | bytes 98308
  10.9 189.8 %copy-start.48 = (f32[64,1,128]{2,1,0:T(1,128)}, f32[64,1,128]{2,1,0:T(1,128)S(1)}, u32[]{:S(2)}) copy-start(f32[64,1,128]{2,1,0:T(1,128)S(1)} %get-tuple-element.142) | copy-start | bytes 98308
  53.7 2.6 collective-permute-start
  55.0 4.8 collective-permute-start.1
  62.3 278.9 %reduce-scatter.4.cloned.1.call-start = ((), (), s32[]{:S(2)}) async-start(), calls=%async_computation.4 | async-start | bytes 5242880 | tf_op jit(solution)/shard_map/reduce_scatter | solution.py:131
  144.5 3.1 collective-permute-start.2
  146.3 4.7 collective-permute-start.3
  246.3 8.7 collective-permute-start.4
  253.0 3.4 collective-permute-start.5
  261.0 220.0 %all-reduce.10.cloned.1.call-start = ((), (), s32[]{:S(2)}) async-start(), calls=%async_computation.11 | async-start | bytes 524288 | tf_op jit(solution)/shard_map/psum | solution.py:58
  354.4 266.0 %all-gather.6.cloned.1.call-start = ((), (), s32[]{:S(2)}) async-start(), calls=%async_computation.5 | async-start | bytes 5242880 | tf_op jit(solution)/shard_map/all_gather | solution.py:117
  540.4 283.0 %reduce-scatter.6.cloned.1.call-start = ((), (), s32[]{:S(2)}) async-start(), calls=%async_computation.6 | async-start | bytes 5242880 | tf_op jit(solution)/shard_map/reduce_scatter | solution.py:131
  621.4 3.1 collective-permute-start.6
  623.2 4.7 collective-permute-start.7
  728.3 8.9 collective-permute-start.8
  735.0 3.4 collective-permute-start.9
  743.0 215.3 %all-reduce.8.cloned.1.call-start = ((), (), s32[]{:S(2)}) async-start(), calls=%async_computation.10 | async-start | bytes 393216 | tf_op jit(solution)/shard_map/psum | solution.py:135
  833.5 242.8 %all-gather.8.cloned.1.call-start = ((), (), s32[]{:S(2)}) async-start(), calls=%async_computation.7 | async-start | bytes 5242880 | tf_op jit(solution)/shard_map/all_gather | solution.py:117
  994.6 290.1 %reduce-scatter.8.cloned.1.call-start = ((), (), s32[]{:S(2)}) async-start(), calls=%async_computation.8 | async-start | bytes 5242880 | tf_op jit(solution)/shard_map/reduce_scatter | solution.py:131
  1077.4 3.2 collective-permute-start.10
  1079.2 4.7 collective-permute-start.11
  1099.3 46.6 %copy-start.4 = (f32[64,128,128]{2,1,0:T(8,128)S(1)}, f32[64,128,128]{2,1,0:T(8,128)}, u32[]{:S(2)}) copy-start(f32[64,128,128]{2,1,0:T(8,128)} %gather_fusion.5) | copy-start | bytes 12582916
  1099.3 46.6 %copy-start.20 = (s32[64,1,128]{2,1,0:T(1,128)S(1)}, s32[64,1,128]{2,1,0:T(1,128)}, u32[]{:S(2)}) copy-start(s32[64,1,128]{2,1,0:T(1,128)} %copy-done.18) | copy-start | bytes 98308
  1099.3 46.6 %copy-start.23 = (s32[64,1,128]{2,1,0:T(1,128)S(1)}, s32[64,1,128]{2,1,0:T(1,128)}, u32[]{:S(2)}) copy-start(s32[64,1,128]{2,1,0:T(1,128)} %copy-done.21) | copy-start | bytes 98308
  1099.3 46.6 %copy-start.26 = (s32[64,1,128]{2,1,0:T(1,128)S(1)}, s32[64,1,128]{2,1,0:T(1,128)}, u32[]{:S(2)}) copy-start(s32[64,1,128]{2,1,0:T(1,128)} %copy-done.24) | copy-start | bytes 98308
  1099.4 46.6 %copy-start.29 = (f32[64,1,128]{2,1,0:T(1,128)S(1)}, f32[64,1,128]{2,1,0:T(1,128)}, u32[]{:S(2)}) copy-start(f32[64,1,128]{2,1,0:T(1,128)} %copy-done.27) | copy-start | bytes 98308
  1099.4 46.6 %copy-start.32 = (f32[64,1,128]{2,1,0:T(1,128)S(1)}, f32[64,1,128]{2,1,0:T(1,128)}, u32[]{:S(2)}) copy-start(f32[64,1,128]{2,1,0:T(1,128)} %copy-done.30) | copy-start | bytes 98308
  1099.4 46.6 %copy-start.35 = (f32[64,1,128]{2,1,0:T(1,128)S(1)}, f32[64,1,128]{2,1,0:T(1,128)}, u32[]{:S(2)}) copy-start(f32[64,1,128]{2,1,0:T(1,128)} %copy-done.33) | copy-start | bytes 98308
  1099.4 46.6 %copy-start.38 = (f32[64,1,128]{2,1,0:T(1,128)S(1)}, f32[64,1,128]{2,1,0:T(1,128)}, u32[]{:S(2)}) copy-start(f32[64,1,128]{2,1,0:T(1,128)} %copy-done.36) | copy-start | bytes 98308
  1189.7 8.9 collective-permute-start.12
  1196.4 3.4 collective-permute-start.13
  1204.5 205.4 %all-reduce.6.cloned.1.call-start = ((), (), s32[]{:S(2)}) async-start(), calls=%async_computation.9 | async-start | bytes 131072 | tf_op jit(solution)/shard_map/psum | solution.py:135
  1288.7 149.5 %copy-start.3 = (f32[2048,128]{1,0:T(8,128)S(1)}, f32[2048,128]{1,0:T(8,128)}, u32[]{:S(2)}) copy-start(f32[2048,128]{1,0:T(8,128)} %convolution_subtract_fusion.1) | copy-start | bytes 3145732
  1291.9 146.2 %copy-start.6 = (f32[2048,128]{1,0:T(8,128)S(1)}, f32[2048,128]{1,0:T(8,128)}, u32[]{:S(2)}) copy-start(f32[2048,128]{1,0:T(8,128)} %reduce-scatter.8.cloned.1.call-done) | copy-start | bytes 3145732
  (27 other events, 336.8 us)
Sparse Core Ops, SparseCore 0:
  62.5 80.9 all-gather.3
  261.2 80.0 reduce-scatter.3
  354.5 126.5 all-reduce.9
  540.6 79.7 all-gather.5
  743.2 80.1 reduce-scatter.5
  833.7 124.6 all-reduce.7
  994.7 81.6 all-gather.7
  1204.6 80.0 reduce-scatter.7
  1291.7 118.0 all-reduce.5
where the time goes:
time: 1450 us
  waiting for transfers between devices  840 us (58%)
  matrix products  313 us (22%)
  other arithmetic  161 us (11%)
  local copies, waits for them, and re-layouts  58.5 us (4%)
  starting transfers between devices  37.7 us (3%)
  blocking collectives  21.2 us (1%)
  between operations  15.5 us (1%)
    all_gather x3, waiting for transfers between devices, body(): group_vec = lax.all_gather(scaled, 'cols', axis=0, tiled=True)  243 us
    psum x2, waiting for transfers between devices, body(): lax.psum((inner_gram(direction, image_vec), inner_gram(image_vec, residua...  232 us
    reduce_scatter x3, waiting for transfers between devices, body(): lax.psum_scatter(graph_middle.reshape(group_rows, query_width), 'cols', s...  222 us
    psum x1, waiting for transfers between devices, residual_square(): return lax.psum(inner_gram(residual, residual), ('nodes', 'cols'))  126 us
    dot_general x3, matrix products, tile_terms(): jnp.einsum('tjr,tjq->trq', dense_tile, pieces[row_safe], precision=HIGH)  122 us
    dot_general x3, matrix products, tile_terms(): jnp.einsum('trj,tjq->trq', dense_tile, pieces[col_safe], precision=HIGH)  102 us
    another operation x15, other arithmetic, solve_gram(): jnp.linalg.cholesky(matrix)  62 us
    another operation x10, other arithmetic, solve_gram(): jax.scipy.linalg.cho_solve((jnp.linalg.cholesky(matrix), True), right_side)  54.1 us
  transfers between devices with their start and end apart: 23, of which 16 were waited for; matrix products, arithmetic and copies ran while one was open for 2% of the time, Pallas kernels for 0%

commit v1 on v0

v1 whole, which is shorter than its diff:
```python
import functools

import jax
import jax.numpy as jnp
from jax import lax
from jax.experimental import pallas as pl
from jax.experimental.pallas import tpu as pltpu
from jax.sharding import PartitionSpec as P

TB = 128
KT = 8
BAND = 4
ITERS = 3
SPAN = 2 * BAND + 1
HALO = BAND * TB
EDGE = BAND * (BAND + 1) // 2

HIGH = lax.Precision.HIGHEST
ALPHA = 0.9
BOOST = 4.0
MESH = pl.DeviceIdType.MESH


def mm(left, right):
    return jnp.dot(left, right, precision=HIGH, preferred_element_type=jnp.float32)


def mm_t(left, right):
    return lax.dot_general(
        left, right, (((0,), (0,)), ((), ())), precision=HIGH, preferred_element_type=jnp.float32
    )


def band_kernel(offsets, tiles_ref, band_ref, inv_ref):
    row = pl.program_id(0)
    places = lax.broadcasted_iota(jnp.int32, (TB, TB), 0).astype(jnp.float32)

    def transposed_tile(offset):
        at = pl.multiple_of(offset, 8)
        ids = tiles_ref[pl.ds(at, KT), :]
        weights = tiles_ref[pl.ds(at + KT, KT), :]
        total = jnp.zeros((TB, TB), jnp.float32)
        for k in range(KT):
            total = total + jnp.where(ids[k : k + 1, :] == places, weights[k : k + 1, :], 0.0)
        return total

    for o in range(SPAN):
        forward = offsets[0, row * SPAN + o]
        backward = offsets[1, row * SPAN + o]
        lanes = slice(o * TB, (o + 1) * TB)

        @pl.when(forward >= 0)
        def _():
            band_ref[:, lanes] = transposed_tile(forward).T

        @pl.when(forward < 0)
        def _():
            band_ref[:, lanes] = jnp.zeros((TB, TB), jnp.float32)

        @pl.when(backward >= 0)
        def _():
            band_ref[:, lanes] += transposed_tile(backward)

    folded = band_ref[:, 0:TB]
    for o in range(1, SPAN):
        folded = folded + band_ref[:, o * TB : (o + 1) * TB]
    degree = jnp.broadcast_to(jnp.sum(folded, axis=1, keepdims=True), (TB, TB))
    root = lax.rsqrt(degree)
    inv_ref[...] = root * (1.5 - 0.5 * degree * root * root)


def build_band(offsets, tiles, row_blocks):
    return pl.pallas_call(
        band_kernel,
        grid_spec=pltpu.PrefetchScalarGridSpec(
            num_scalar_prefetch=1,
            grid=(row_blocks,),
            in_specs=[pl.BlockSpec(tiles.shape, lambda i, _: (0, 0))],
            out_specs=[
                pl.BlockSpec((TB, SPAN * TB), lambda i, _: (i, 0)),
                pl.BlockSpec((TB, TB), lambda i, _: (i, 0)),
            ],
        ),
        out_shape=[
            jax.ShapeDtypeStruct((row_blocks * TB, SPAN * TB), jnp.float32),
            jax.ShapeDtypeStruct((row_blocks * TB, TB), jnp.float32),
        ],
        compiler_params=pltpu.CompilerParams(vmem_limit_bytes=32 * 1024 * 1024),
    )(offsets, tiles)


def flipped(index, bit):
    return index + bit - 2 * bit * ((index // bit) % 2)


def cg_kernel(
    nodes, cols, prior_ref, queries_ref, band_ref, inv_ref, x_ref, r_ref,
    vext, direc, image, wbuf, acc, slots, pair, curv_old, ratio_ref, step_ref,
    halo_send, halo_recv, sum_send, sum_recv,
):
    rows = prior_ref.shape[0]
    blocks = rows // TB
    node = lax.axis_index("nodes")
    col = lax.axis_index("cols")
    right = ((node + (col + 1) // cols) % nodes, (col + 1) % cols)
    left = ((node + nodes - 1 + (col + cols - 1) // cols) % nodes, (col + cols - 1) % cols)
    partners = []
    bit = 1
    while bit < nodes:
        partners.append((flipped(node, bit), col))
        bit *= 2
    bit = 1
    while bit < cols:
        partners.append((node, flipped(col, bit)))
        bit *= 2
    stages = len(partners)

    barrier = pltpu.get_barrier_semaphore()
    for other in [left, right] + partners:
        pl.semaphore_signal(barrier, inc=1, device_id=other, device_id_type=MESH)

    base = (node * cols + col) * rows
    chunk = 2 * TB

    def start_rows(c, carry):
        at = pl.ds(pl.multiple_of(c * chunk, chunk), chunk)
        where_at = base + c * chunk + lax.broadcasted_iota(jnp.int32, (chunk, TB), 0)
        r_ref[at, :] = prior_ref[at, :] + jnp.where(where_at == queries_ref[...], BOOST, 0.0)
        x_ref[at, :] = jnp.zeros((chunk, TB), jnp.float32)
        direc[at, :] = jnp.zeros((chunk, TB), jnp.float32)
        image[at, :] = jnp.zeros((chunk, TB), jnp.float32)
        return carry

    lax.fori_loop(0, rows // chunk, start_rows, 0)
    pair[...] = jnp.zeros_like(pair)
    curv_old[...] = jnp.zeros_like(curv_old)
    lane = lax.broadcasted_iota(jnp.int32, (TB, TB), 1)
    lane_row = lax.broadcasted_iota(jnp.int32, (1, TB), 1)
    pl.semaphore_wait(barrier, stages + 2)

    def iteration(it, carry):
        def scale_rows(c, inner):
            at = pl.multiple_of(c * chunk, chunk)
            vext[it, pl.ds(HALO + at, chunk), :] = inv_ref[pl.ds(at, chunk), :] * r_ref[pl.ds(at, chunk), :]
            return inner

        lax.fori_loop(0, rows // chunk, scale_rows, 0)
        to_right = pltpu.make_async_remote_copy(
            src_ref=vext.at[it, pl.ds(rows, HALO), :],
            dst_ref=vext.at[it, pl.ds(0, HALO), :],
            send_sem=halo_send.at[2 * it], recv_sem=halo_recv.at[2 * it],
            device_id=right, device_id_type=MESH,
        )
        to_left = pltpu.make_async_remote_copy(
            src_ref=vext.at[it, pl.ds(HALO, HALO), :],
            dst_ref=vext.at[it, pl.ds(HALO + rows, HALO), :],
            send_sem=halo_send.at[2 * it + 1], recv_sem=halo_recv.at[2 * it + 1],
            device_id=left, device_id_type=MESH,
        )
        to_right.start()
        to_left.start()

        def apply_block(b, inner):
            at = pl.multiple_of(b * TB, TB)
            product = mm(band_ref[pl.ds(at, TB), :], vext[it, pl.ds(at, SPAN * TB), :])
            mine = pl.ds(at, TB)
            wbuf[mine, :] = r_ref[mine, :] - ALPHA * inv_ref[mine, :] * product
            return inner

        lax.fori_loop(BAND, blocks - BAND, apply_block, 0)
        to_right.wait()
        to_left.wait()
        lax.fori_loop(0, BAND, apply_block, 0)
        lax.fori_loop(blocks - BAND, blocks, apply_block, 0)

        acc[...] = jnp.zeros_like(acc)

        def add_gram(c, inner):
            at = pl.ds(pl.multiple_of(c * chunk, chunk), chunk)
            part = r_ref[at, :]
            acc[...] += mm_t(part, jnp.concatenate([part, wbuf[at, :]], axis=1))
            return inner

        lax.fori_loop(0, rows // chunk, add_gram, 0)
        for stage, other in enumerate(partners):
            spot = it * stages + stage
            copy = pltpu.make_async_remote_copy(
                src_ref=acc, dst_ref=slots.at[spot],
                send_sem=sum_send.at[spot], recv_sem=sum_recv.at[spot],
                device_id=other, device_id_type=MESH,
            )
            copy.start()
            copy.wait()
            acc[...] += slots[spot]

        gram = acc[:, 0:TB]
        ratio = mm(pair[0], gram)
        ratio_ref[...] = ratio
        curvature = acc[:, TB : 2 * TB] - mm_t(ratio, mm(curv_old[...], ratio))
        curv_old[...] = curvature
        pair[0] = gram
        pair[1] = curvature

        def pivot(k, inner):
            for j in range(2):
                whole = pair[j]
                line = pair[j, pl.ds(k, 1), :]
                hit = lane == k
                hit_row = lane_row == k
                column = jnp.sum(jnp.where(hit, whole, 0.0), axis=1, keepdims=True)
                corner = jnp.sum(jnp.where(hit_row, line, 0.0), axis=1, keepdims=True)
                scaled = jnp.where(hit_row, 1.0, line) / corner
                pair[j] = jnp.where(hit, 0.0, whole) - column * scaled
                pair[j, pl.ds(k, 1), :] = scaled
            return inner

        lax.fori_loop(0, TB, pivot, 0)
        step_ref[...] = mm(pair[1], acc[:, 0:TB])

        def update_rows(c, inner):
            at = pl.ds(pl.multiple_of(c * chunk, chunk), chunk)
            fresh = r_ref[at, :] + mm(direc[at, :], ratio_ref[...])
            direc[at, :] = fresh
            x_ref[at, :] += mm(fresh, step_ref[...])
            turned = wbuf[at, :] + mm(image[at, :], ratio_ref[...])
            image[at, :] = turned
            r_ref[at, :] -= mm(turned, step_ref[...])
            return inner

        lax.fori_loop(0, rows // chunk, update_rows, 0)
        return carry

    lax.fori_loop(0, ITERS, iteration, 0)


def run_cg(nodes, cols, prior, queries, band, inv):
    rows = prior.shape[0]
    stages = (nodes.bit_length() - 1) + (cols.bit_length() - 1)
    full = pl.BlockSpec(memory_space=pltpu.VMEM)
    shape = jax.ShapeDtypeStruct((rows, TB), jnp.float32)
    big = pltpu.VMEM((rows, TB), jnp.float32)
    small = pltpu.VMEM((TB, TB), jnp.float32)
    return pl.pallas_call(
        functools.partial(cg_kernel, nodes, cols),
        in_specs=[full] * 4,
        out_specs=[full] * 2,
        out_shape=[shape, shape],
        scratch_shapes=[
            pltpu.VMEM((ITERS, rows + 2 * HALO, TB), jnp.float32),
            big, big, big,
            pltpu.VMEM((TB, 2 * TB), jnp.float32),
            pltpu.VMEM((ITERS * stages, TB, 2 * TB), jnp.float32),
            pltpu.VMEM((2, TB, TB), jnp.float32),
            small, small, small,
            pltpu.SemaphoreType.DMA((2 * ITERS,)),
            pltpu.SemaphoreType.DMA((2 * ITERS,)),
            pltpu.SemaphoreType.DMA((ITERS * stages,)),
            pltpu.SemaphoreType.DMA((ITERS * stages,)),
        ],
        compiler_params=pltpu.CompilerParams(
            collective_id=0, has_side_effects=True, vmem_limit_bytes=56 * 1024 * 1024
        ),
    )(prior, queries, band, inv)


def body(prior, queries, tile_rows, tile_cols, tile_ids, tile_weights):
    rows_dev = prior.shape[0]
    nodes = lax.axis_size("nodes")
    cols = lax.axis_size("cols")
    node = lax.axis_index("nodes")
    member = lax.axis_index("cols")
    per_dev = tile_rows.shape[0]
    row_blocks = rows_dev // TB
    blocks = row_blocks * cols
    first = node * blocks

    keys = jnp.where(
        tile_rows >= 0, (tile_rows - first) * SPAN + (tile_cols - tile_rows + BAND), -1
    ).astype(jnp.float32)
    packed = jnp.concatenate([tile_ids.astype(jnp.float32), tile_weights], axis=1)
    meta_rows = 8 * (-(-per_dev // (8 * TB)))
    meta = jnp.full((meta_rows * TB,), -1.0, jnp.float32).at[:per_dev].set(keys)
    flat = jnp.concatenate([packed.reshape(per_dev * 2 * KT, TB), meta.reshape(meta_rows, TB)])
    gathered = lax.all_gather(flat, "cols", axis=0, tiled=False)
    stride = flat.shape[0]
    slot_keys = gathered[:, per_dev * 2 * KT :, :].reshape(cols, -1)[:, :per_dev].reshape(-1).astype(jnp.int32)
    slot = jnp.arange(cols * per_dev, dtype=jnp.int32)
    slot_at = (slot // per_dev) * stride + (slot % per_dev) * 2 * KT

    def find(wanted):
        return jnp.max(
            jnp.where(wanted[:, None] == slot_keys[None, :], slot_at[None, :], -1), axis=1
        )

    far = [a for a in range(BAND) for _ in range(a + 1)]
    near = [c for a in range(BAND) for c in range(a + 1)]
    far = jnp.array(far, jnp.int32)
    near = jnp.array(near, jnp.int32)
    up_keys = (blocks - BAND + far) * SPAN + (2 * BAND + near - far)
    down_keys = near * SPAN + (far - near)
    group_tiles = gathered.reshape(cols * stride, TB)

    def pick(wanted):
        at = find(wanted)
        found = jnp.maximum(at, 0)[:, None] + jnp.arange(2 * KT, dtype=jnp.int32)[None, :]
        chosen = group_tiles[found]
        return jnp.where((at >= 0)[:, None, None], chosen, 0.0).reshape(EDGE * 2 * KT, TB)

    from_prev = lax.ppermute(pick(up_keys), "nodes", [(i, i + 1) for i in range(nodes - 1)])
    from_next = lax.ppermute(pick(down_keys), "nodes", [(i + 1, i) for i in range(nodes - 1)])
    tiles = jnp.concatenate([group_tiles, from_prev, from_next])

    place = jnp.arange(row_blocks * SPAN, dtype=jnp.int32)
    i_at = member * row_blocks + place // SPAN
    o_at = place % SPAN
    forward = find(i_at * SPAN + o_at)
    back_row = i_at + o_at - BAND
    inside = find(back_row * SPAN + 2 * BAND - o_at)
    edge_at = cols * stride
    a_prev = back_row + BAND
    prev_at = edge_at + (a_prev * (a_prev + 1) // 2 + i_at) * 2 * KT
    c_next = i_at - (blocks - BAND)
    next_at = edge_at + (EDGE + c_next * (c_next + 1) // 2 + back_row - blocks) * 2 * KT
    backward = jnp.where(back_row < 0, prev_at, jnp.where(back_row >= blocks, next_at, inside))
    band, inv = build_band(jnp.stack([forward, backward]), tiles, row_blocks)
    return tuple(run_cg(nodes, cols, prior, queries[None, :], band, inv))


def solution(mesh):
    in_specs = (
        P(("nodes", "cols"), None),
        P(),
        P(("nodes", "cols")),
        P(("nodes", "cols")),
        P(("nodes", "cols"), None, None),
        P(("nodes", "cols"), None, None),
    )
    out_specs = (P(("nodes", "cols"), None), P(("nodes", "cols"), None))
    return jax.shard_map(body, mesh=mesh, in_specs=in_specs, out_specs=out_specs, check_vma=False)
```

time: 1450 us -> 335 us (0.23)
  waiting for transfers between devices: 840 us -> 50 us
  matrix products: 313 us -> 0 us
  Pallas kernels: 0 us -> 246 us
  other arithmetic: 161 us -> 6.04 us
  local copies, waits for them, and re-layouts: 58.5 us -> 13.8 us
  starting transfers between devices: 37.7 us -> 4.36 us
  blocking collectives: 21.2 us -> 0 us
    psum x3 -> x0, waiting for transfers between devices: 358 us -> none  [the longest x2 232 us: body(): lax.psum((inner_gram(direction, image_vec), inner_gram(image_vec, residua...]
    dot_general x36 -> x0, matrix products: 310 us -> none  [the longest x3 122 us: tile_terms(): jnp.einsum('tjr,tjq->trq', dense_tile, pieces[row_safe], precision=HIGH)]
    pallas_call x0 -> x2, Pallas kernels: none -> 246 us  [the longest x1 230 us: run_cg(): pl.pallas_call(functools.partial(cg_kernel, nodes, cols), in_specs=[full]...]
    reduce_scatter x3 -> x0, waiting for transfers between devices: 222 us -> none  [body(): lax.psum_scatter(graph_middle.reshape(group_rows, query_width), 'cols', s...]
    all_gather x3 -> x1, waiting for transfers between devices: 243 us -> 49.1 us  [body(): gathered = lax.all_gather(flat, 'cols', axis=0, tiled=False)]
    another operation x25 -> x1, other arithmetic: 116 us -> 0.01 us  [body(): band, inv = build_band(jnp.stack([forward, backward]), tiles, row_blocks)]
    ppermute x14 -> x2, starting transfers between devices: 36.4 us -> 4.33 us  [the longest x1 3.03 us: body(): lax.ppermute(pick(up_keys), 'nodes', [(i, i + 1) for i in range(nodes - 1)])]
    gather x6 -> x2, local copies, waits for them, and re-layouts: 31.5 us -> 4.53 us  [pick(): chosen = group_tiles[found]]
  transfers between devices with their start and end apart: 23 -> 3, of which waited for: 16 -> 2; matrix products, arithmetic and copies ran while one was open for 2% -> 1% of each run, Pallas kernels for 0% -> 0%
where the time goes in v1:
time: 335 us; the launch traced here: 334 us
  Pallas kernels  246 us (73%)
  waiting for transfers between devices  50 us (15%)
  between operations  14.2 us (4%)
  local copies, waits for them, and re-layouts  13.8 us (4%)
  other arithmetic  6.04 us (2%)
  starting transfers between devices  4.36 us (1%)
    pallas_call x1, Pallas kernels, run_cg(): pl.pallas_call(functools.partial(cg_kernel, nodes, cols), in_specs=[full]...  230 us
    all_gather x1, waiting for transfers between devices, body(): gathered = lax.all_gather(flat, 'cols', axis=0, tiled=False)  49.1 us
    pallas_call x1, Pallas kernels, build_band(): pl.pallas_call(band_kernel, grid_spec=pltpu.PrefetchScalarGridSpec(num_sc...  15.6 us
    unnamed x14, local copies, waits for them, and re-layouts  8.64 us
  transfers between devices with their start and end apart: 3, of which 2 were waited for; matrix products, arithmetic and copies ran while one was open for 1% of the time, Pallas kernels for 0%

profile of v1, /device:TPU:0, one launch (start us, length us, event | category | flops | bytes accessed | tf_op | source)
XLA Modules:
  0.0 334.0 jit_solution(18021366765825419954)
XLA Ops:
  7.2 0.0 copy-start.3
  7.2 0.0 copy-start.4
  7.2 0.0 all-gather.3.cloned.1.call-start
  7.2 0.7 fusion.10
  7.9 1.0 convert_element_type.16
  8.9 1.0 pad_maximum_fusion.2
  9.9 0.8 pad_maximum_fusion.1
  10.7 0.0 all-gather.3.cloned.1.call-update
  10.8 49.1 %all-gather.3.cloned.1.call-done = f32[4128,128]{1,0:T(8,128)} async-done(((f32[1032,128]{1,0:T(8,128)}), f32[4128,128]{1,0:T(8,128)}) %all-gather.3.cloned.1.call-update) | async-done | bytes 2113552 | tf_op jit(solution)/shard_map/all_gather | solution.py:284
  59.9 0.7 slice_bitcast_fusion
  60.6 0.1 convert_element_type.19
  60.7 0.0 copy-done.3
  60.7 0.0 copy-done.4
  60.7 0.2 select_reduce_fusion.3
  60.9 0.2 select_reduce_fusion.1
  61.2 0.1 broadcast_in_dim.100
  61.2 0.1 broadcast_in_dim.101
  61.3 0.1 broadcast_in_dim.96
  61.4 0.1 broadcast_in_dim.97
  61.5 0.1 compare_select_fusion
  61.6 0.1 reshape.408
  61.7 0.1 compare_select_fusion.1
  61.7 0.1 reshape.400
  61.8 2.3 gather_fusion.1
  64.1 0.1 broadcast_select_fusion
  64.2 1.3 collective-permute-start.1
  65.5 2.3 gather_fusion
  67.8 0.1 broadcast_select_fusion.1
  67.9 3.0 collective-permute-start
  70.9 0.0 collective-permute-done.1
  70.9 0.9 collective-permute-done
  71.8 1.7 pad_maximum_fusion.tiles_ref
  73.6 15.6 %shard_map.95 = (f32[2048,1152]{1,0:T(8,128)S(1)}, f32[2048,128]{1,0:T(8,128)S(1)}) custom-call(s32[2,144]{1,0:T(2,128)S(1)} %pad_add_fusion.offsets, f32[4448,128]{1,0:T(8,128)S(1)} %pad_maximum_fusion.tiles_ref), custom_call_target="tpu_custom_call" | custom-call | tf_op jit(solution)/shard_map/pallas_call | solution.py:73
  89.1 0.0 copy-start
  89.1 3.6 %copy-done = f32[2048,1152]{1,0:T(8,128)} copy-done((f32[2048,1152]{1,0:T(8,128)}, f32[2048,1152]{1,0:T(8,128)S(1)}, u32[]{:S(2)}) %copy-start) | copy-done | bytes 9437208
  92.7 0.0 copy-start.1
  92.7 1.0 copy-done.1
  93.7 230.1 %shard_map.96 = (f32[2048,128]{1,0:T(8,128)}, f32[2048,128]{1,0:T(8,128)}) custom-call(f32[2048,128]{1,0:T(8,128)} %prior_ref.1, s32[1,128]{1,0:T(1,128)} %bitcast.21, f32[2048,1152]{1,0:T(8,128)} %copy-done, f32[2048,128]{1,0:T(8,128)} %copy-done.1), custom_call_target="tpu_custom_call" | custom-call | tf_op jit(solution)/shard_map/pallas_call | solution.py:243
  323.9 0.0 copy-start.2
  323.9 2.4 copy.15
  326.2 0.0 copy-done.2
  326.2 1.0 copy.16
  (11 shorter events, 0.1 us)
Async XLA Ops:
  7.2 53.5 %copy-start.3 = (s32[10]{0:T(128)S(1)}, s32[10]{0:T(128)}, u32[]{:S(2)}) copy-start(s32[10]{0:T(128)} %constant.163) | copy-start | bytes 124
  7.2 53.5 %copy-start.4 = (s32[10]{0:T(128)S(1)}, s32[10]{0:T(128)}, u32[]{:S(2)}) copy-start(s32[10]{0:T(128)} %constant.160) | copy-start | bytes 124
  7.2 52.7 %all-gather.3.cloned.1.call-start = ((), (), s32[]{:S(2)}) async-start(), calls=%async_computation | async-start | bytes 2641920 | tf_op jit(solution)/shard_map/all_gather | solution.py:284
  64.2 6.7 %collective-permute-start.1 = (f32[160,128]{1,0:T(8,128)S(1)}, f32[160,128]{1,0:T(8,128)S(1)}, u32[]{:S(2)}, u32[]{:S(2)}) collective-permute-start(f32[160,128]{1,0:T(8,128)S(1)} %broadcast_select_fusion), channel_id=1, source_target_pairs={{4,0},{8,4},{12,8},{16,12},{20,16},{24,20},{28,24},{5,1},{9,5},{13... | collective-permute-start | bytes 245768 | tf_op jit(solution)/shard_map/ppermute | solution.py:310
  67.9 3.9 %collective-permute-start = (f32[160,128]{1,0:T(8,128)S(1)}, f32[160,128]{1,0:T(8,128)S(1)}, u32[]{:S(2)}, u32[]{:S(2)}) collective-permute-start(f32[160,128]{1,0:T(8,128)S(1)} %broadcast_select_fusion.1), channel_id=1, source_target_pairs={{0,4},{4,8},{8,12},{12,16},{16,20},{20,24},{24,28},{1,5},{5,9},{9,... | collective-permute-start | bytes 245768 | tf_op jit(solution)/shard_map/ppermute | solution.py:309
  89.1 3.6 %copy-start = (f32[2048,1152]{1,0:T(8,128)}, f32[2048,1152]{1,0:T(8,128)S(1)}, u32[]{:S(2)}) copy-start(f32[2048,1152]{1,0:T(8,128)S(1)} %get-tuple-element.16.band_ref) | copy-start | bytes 28311556
  92.7 1.0 copy-start.1
  323.9 2.4 copy-start.2
Sparse Core Ops, SparseCore 0:
  10.9 48.9 all-gather.2

commit v2 on v1

--- a/solution.py
+++ b/solution.py
@@ -89,14 +89,48 @@
     )(offsets, tiles)
 
 
-def flipped(index, bit):
-    return index + bit - 2 * bit * ((index // bit) % 2)
+def invert_in_place(matrix):
+    lane = lax.broadcasted_iota(jnp.int32, (TB, TB), 1)
+    lane_row = lax.broadcasted_iota(jnp.int32, (1, TB), 1)
+
+    def entry(line, k):
+        return jnp.sum(jnp.where(lane_row == k, line, 0.0), axis=1, keepdims=True)
+
+    def pivot(m, carry):
+        k = 2 * m
+        whole = matrix[...]
+        first = matrix[pl.ds(k, 1), :]
+        second = matrix[pl.ds(k + 1, 1), :]
+        hit0 = lane == k
+        hit1 = lane == k + 1
+        column0 = jnp.sum(jnp.where(hit0, whole, 0.0), axis=1, keepdims=True)
+        column1 = jnp.sum(jnp.where(hit1, whole, 0.0), axis=1, keepdims=True)
+        rest = jnp.where(hit0 | hit1, 0.0, whole)
+        a = entry(first, k)
+        b = entry(first, k + 1)
+        c = entry(second, k)
+        d = entry(second, k + 1)
+        inv_a = 1.0 / a
+        lower = c * inv_a
+        upper = b * inv_a
+        inv_s = 1.0 / (d - c * upper)
+        row0 = jnp.where(lane_row == k, 1.0, jnp.where(lane_row == k + 1, 0.0, first))
+        row1 = jnp.where(lane_row == k, 0.0, jnp.where(lane_row == k + 1, 1.0, second))
+        new1 = (row1 - lower * row0) * inv_s
+        new0 = row0 * inv_a - upper * new1
+        matrix[...] = rest - column0 * new0 - column1 * new1
+        matrix[pl.ds(k, 1), :] = new0
+        matrix[pl.ds(k + 1, 1), :] = new1
+        return carry
+
+    lax.fori_loop(0, TB // 2, pivot, 0)
 
 
 def cg_kernel(
     nodes, cols, prior_ref, queries_ref, band_ref, inv_ref, x_ref, r_ref,
-    vext, direc, image, wbuf, acc, slots, pair, curv_old, ratio_ref, step_ref,
-    halo_send, halo_recv, sum_send, sum_recv,
+    vext, direc, image, wbuf, acc, spread, column_sums, total, gram_inv, curv_inv, curv_old,
+    ratio_ref, step_ref, halo_send, halo_recv, spread_send, spread_recv, col_send, col_recv,
+    back_send, back_recv,
 ):
     rows = prior_ref.shape[0]
     blocks = rows // TB
@@ -104,47 +138,41 @@
     col = lax.axis_index("cols")
     right = ((node + (col + 1) // cols) % nodes, (col + 1) % cols)
     left = ((node + nodes - 1 + (col + cols - 1) // cols) % nodes, (col + cols - 1) % cols)
-    partners = []
-    bit = 1
-    while bit < nodes:
-        partners.append((flipped(node, bit), col))
-        bit *= 2
-    bit = 1
-    while bit < cols:
-        partners.append((node, flipped(col, bit)))
-        bit *= 2
-    stages = len(partners)
+    share = 2 * TB // nodes
+
+    def node_at(k):
+        return (node + k) % nodes
+
+    def col_at(k):
+        return (col + k) % cols
 
     barrier = pltpu.get_barrier_semaphore()
-    for other in [left, right] + partners:
+    others = [left, right]
+    others += [(node_at(k), col) for k in range(1, nodes)]
+    others += [(node, col_at(k)) for k in range(1, cols)]
+    for other in others:
         pl.semaphore_signal(barrier, inc=1, device_id=other, device_id_type=MESH)
 
     base = (node * cols + col) * rows
     chunk = 2 * TB
 
     def start_rows(c, carry):
-        at = pl.ds(pl.multiple_of(c * chunk, chunk), chunk)
+        start = pl.multiple_of(c * chunk, chunk)
+        at = pl.ds(start, chunk)
         where_at = base + c * chunk + lax.broadcasted_iota(jnp.int32, (chunk, TB), 0)
-        r_ref[at, :] = prior_ref[at, :] + jnp.where(where_at == queries_ref[...], BOOST, 0.0)
+        target = prior_ref[at, :] + jnp.where(where_at == queries_ref[...], BOOST, 0.0)
+        r_ref[at, :] = target
+        vext[0, pl.ds(HALO + start, chunk), :] = inv_ref[at, :] * target
         x_ref[at, :] = jnp.zeros((chunk, TB), jnp.float32)
         direc[at, :] = jnp.zeros((chunk, TB), jnp.float32)
         image[at, :] = jnp.zeros((chunk, TB), jnp.float32)
         return carry
 
     lax.fori_loop(0, rows // chunk, start_rows, 0)
-    pair[...] = jnp.zeros_like(pair)
+    gram_inv[...] = jnp.zeros_like(gram_inv)
     curv_old[...] = jnp.zeros_like(curv_old)
-    lane = lax.broadcasted_iota(jnp.int32, (TB, TB), 1)
-    lane_row = lax.broadcasted_iota(jnp.int32, (1, TB), 1)
-    pl.semaphore_wait(barrier, stages + 2)
-
-    def iteration(it, carry):
-        def scale_rows(c, inner):
-            at = pl.multiple_of(c * chunk, chunk)
-            vext[it, pl.ds(HALO + at, chunk), :] = inv_ref[pl.ds(at, chunk), :] * r_ref[pl.ds(at, chunk), :]
-            return inner
-
-        lax.fori_loop(0, rows // chunk, scale_rows, 0)
+
+    def halo(it):
         to_right = pltpu.make_async_remote_copy(
             src_ref=vext.at[it, pl.ds(rows, HALO), :],
             dst_ref=vext.at[it, pl.ds(0, HALO), :],
@@ -157,9 +185,13 @@
             send_sem=halo_send.at[2 * it + 1], recv_sem=halo_recv.at[2 * it + 1],
             device_id=left, device_id_type=MESH,
         )
-        to_right.start()
-        to_left.start()
-
+        return to_right, to_left
+
+    pl.semaphore_wait(barrier, len(others))
+    for copy in halo(0):
+        copy.start()
+
+    def iteration(it, carry):
         def apply_block(b, inner):
             at = pl.multiple_of(b * TB, TB)
             product = mm(band_ref[pl.ds(at, TB), :], vext[it, pl.ds(at, SPAN * TB), :])
@@ -168,8 +200,14 @@
             return inner
 
         lax.fori_loop(BAND, blocks - BAND, apply_block, 0)
-        to_right.wait()
-        to_left.wait()
+
+        @pl.when(it > 0)
+        def _():
+            gram_inv[...] = total[0:TB, :]
+            invert_in_place(gram_inv)
+
+        for copy in halo(it):
+            copy.wait()
         lax.fori_loop(0, BAND, apply_block, 0)
         lax.fori_loop(blocks - BAND, blocks, apply_block, 0)
 
@@ -178,56 +216,94 @@
         def add_gram(c, inner):
             at = pl.ds(pl.multiple_of(c * chunk, chunk), chunk)
             part = r_ref[at, :]
-            acc[...] += mm_t(part, jnp.concatenate([part, wbuf[at, :]], axis=1))
+            both = mm_t(part, jnp.concatenate([part, wbuf[at, :]], axis=1))
+            acc[0:TB, :] += both[:, 0:TB]
+            acc[TB : 2 * TB, :] += both[:, TB : 2 * TB]
             return inner
 
         lax.fori_loop(0, rows // chunk, add_gram, 0)
-        for stage, other in enumerate(partners):
-            spot = it * stages + stage
+
+        own = pl.ds(pl.multiple_of(node * share, share), share)
+        copies = []
+        for k in range(1, nodes):
+            spot = it * nodes + k
             copy = pltpu.make_async_remote_copy(
-                src_ref=acc, dst_ref=slots.at[spot],
-                send_sem=sum_send.at[spot], recv_sem=sum_recv.at[spot],
-                device_id=other, device_id_type=MESH,
+                src_ref=acc.at[pl.ds(pl.multiple_of(node_at(k) * share, share), share), :],
+                dst_ref=spread.at[spot],
+                send_sem=spread_send.at[spot], recv_sem=spread_recv.at[spot],
+                device_id=(node_at(k), col), device_id_type=MESH,
             )
             copy.start()
+            copies.append(copy)
+        for copy in copies:
             copy.wait()
-            acc[...] += slots[spot]
-
-        gram = acc[:, 0:TB]
-        ratio = mm(pair[0], gram)
+        mine = acc[own, :]
+        for k in range(1, nodes):
+            mine = mine + spread[it * nodes + k]
+        column_sums[it * cols + col] = mine
+        copies = []
+        for k in range(1, cols):
+            spot = it * cols + k
+            copy = pltpu.make_async_remote_copy(
+                src_ref=column_sums.at[it * cols + col],
+                dst_ref=column_sums.at[it * cols + col],
+                send_sem=col_send.at[spot], recv_sem=col_recv.at[spot],
+                device_id=(node, col_at(k)), device_id_type=MESH,
+            )
+            copy.start()
+            copies.append(copy)
+        for copy in copies:
+            copy.wait()
+        mine = column_sums[it * cols]
+        for k in range(1, cols):
+            mine = mine + column_sums[it * cols + k]
+        total[own, :] = mine
+        copies = []
+        for k in range(1, nodes):
+            spot = it * nodes + k
+            copy = pltpu.make_async_remote_copy(
+                src_ref=total.at[own, :],
+                dst_ref=total.at[own, :],
+                send_sem=back_send.at[spot], recv_sem=back_recv.at[spot],
+                device_id=(node_at(k), col), device_id_type=MESH,
+            )
+            copy.start()
+            copies.append(copy)
+        for copy in copies:
+            copy.wait()
+
+        gram = total[0:TB, :]
+        ratio = mm(gram_inv[...], gram)
         ratio_ref[...] = ratio
-        curvature = acc[:, TB : 2 * TB] - mm_t(ratio, mm(curv_old[...], ratio))
+        curvature = total[TB : 2 * TB, :] - mm_t(ratio, mm(curv_old[...], ratio))
         curv_old[...] = curvature
-        pair[0] = gram
-        pair[1] = curvature
-
-        def pivot(k, inner):
-            for j in range(2):
-                whole = pair[j]
-                line = pair[j, pl.ds(k, 1), :]
-                hit = lane == k
-                hit_row = lane_row == k
-                column = jnp.sum(jnp.where(hit, whole, 0.0), axis=1, keepdims=True)
-                corner = jnp.sum(jnp.where(hit_row, line, 0.0), axis=1, keepdims=True)
-                scaled = jnp.where(hit_row, 1.0, line) / corner
-                pair[j] = jnp.where(hit, 0.0, whole) - column * scaled
-                pair[j, pl.ds(k, 1), :] = scaled
-            return inner
-
-        lax.fori_loop(0, TB, pivot, 0)
-        step_ref[...] = mm(pair[1], acc[:, 0:TB])
+        curv_inv[...] = curvature
+        invert_in_place(curv_inv)
+        step_ref[...] = mm(curv_inv[...], total[0:TB, :])
 
         def update_rows(c, inner):
-            at = pl.ds(pl.multiple_of(c * chunk, chunk), chunk)
+            start = pl.multiple_of(c * chunk, chunk)
+            at = pl.ds(start, chunk)
             fresh = r_ref[at, :] + mm(direc[at, :], ratio_ref[...])
             direc[at, :] = fresh
             x_ref[at, :] += mm(fresh, step_ref[...])
             turned = wbuf[at, :] + mm(image[at, :], ratio_ref[...])
             image[at, :] = turned
-            r_ref[at, :] -= mm(turned, step_ref[...])
+            left_over = r_ref[at, :] - mm(turned, step_ref[...])
+            r_ref[at, :] = left_over
+            vext[it + 1, pl.ds(HALO + start, chunk), :] = inv_ref[at, :] * left_over
             return inner
 
-        lax.fori_loop(0, rows // chunk, update_rows, 0)
+        edge = HALO // chunk
+        lax.fori_loop(0, edge, update_rows, 0)
+        lax.fori_loop(rows // chunk - edge, rows // chunk, update_rows, 0)
+
+        @pl.when(it < ITERS - 1)
+        def _():
+            for copy in halo(it + 1):
+                copy.start()
+
+        lax.fori_loop(edge, rows // chunk - edge, update_rows, 0)
         return carry
 
     lax.fori_loop(0, ITERS, iteration, 0)
@@ -235,28 +311,28 @@
 
 def run_cg(nodes, cols, prior, queries, band, inv):
     rows = prior.shape[0]
-    stages = (nodes.bit_length() - 1) + (cols.bit_length() - 1)
+    share = 2 * TB // nodes
     full = pl.BlockSpec(memory_space=pltpu.VMEM)
     shape = jax.ShapeDtypeStruct((rows, TB), jnp.float32)
     big = pltpu.VMEM((rows, TB), jnp.float32)
     small = pltpu.VMEM((TB, TB), jnp.float32)
+    tall = pltpu.VMEM((2 * TB, TB), jnp.float32)
     return pl.pallas_call(
         functools.partial(cg_kernel, nodes, cols),
         in_specs=[full] * 4,
         out_specs=[full] * 2,
         out_shape=[shape, shape],
         scratch_shapes=[
-            pltpu.VMEM((ITERS, rows + 2 * HALO, TB), jnp.float32),
-            big, big, big,
-            pltpu.VMEM((TB, 2 * TB), jnp.float32),
-            pltpu.VMEM((ITERS * stages, TB, 2 * TB), jnp.float32),
-            pltpu.VMEM((2, TB, TB), jnp.float32),
-            small, small, small,
-            pltpu.SemaphoreType.DMA((2 * ITERS,)),
-            pltpu.SemaphoreType.DMA((2 * ITERS,)),
-            pltpu.SemaphoreType.DMA((ITERS * stages,)),
-            pltpu.SemaphoreType.DMA((ITERS * stages,)),
-        ],
+            pltpu.VMEM((ITERS + 1, rows + 2 * HALO, TB), jnp.float32),
+            big, big, big, tall,
+            pltpu.VMEM((ITERS * nodes, share, TB), jnp.float32),
+            pltpu.VMEM((ITERS * cols, share, TB), jnp.float32),
+            tall, small, small, small, small, small,
+        ]
+        + [pltpu.SemaphoreType.DMA((2 * ITERS,))] * 2
+        + [pltpu.SemaphoreType.DMA((ITERS * nodes,))] * 2
+        + [pltpu.SemaphoreType.DMA((ITERS * cols,))] * 2
+        + [pltpu.SemaphoreType.DMA((ITERS * nodes,))] * 2,
         compiler_params=pltpu.CompilerParams(
             collective_id=0, has_side_effects=True, vmem_limit_bytes=56 * 1024 * 1024
         ),

time: 335 us -> 258 us (0.77)
  Pallas kernels: 246 us -> 169 us
    pallas_call x1, Pallas kernels: 230 us -> 153 us  [run_cg(): pl.pallas_call(functools.partial(cg_kernel, nodes, cols), in_specs=[full]...]
where the time goes in v2:
time: 258 us
  Pallas kernels  169 us (66%)
  waiting for transfers between devices  50 us (19%)
  between operations  14.2 us (6%)
  local copies, waits for them, and re-layouts  13.8 us (5%)
  other arithmetic  6.04 us (2%)
  starting transfers between devices  4.37 us (2%)
    pallas_call x1, Pallas kernels, run_cg(): pl.pallas_call(functools.partial(cg_kernel, nodes, cols), in_specs=[full]...  153 us
    all_gather x1, waiting for transfers between devices, body(): gathered = lax.all_gather(flat, 'cols', axis=0, tiled=False)  49.1 us
    pallas_call x1, Pallas kernels, build_band(): pl.pallas_call(band_kernel, grid_spec=pltpu.PrefetchScalarGridSpec(num_sc...  16.6 us
    unnamed x14, local copies, waits for them, and re-layouts  8.64 us
  transfers between devices with their start and end apart: 3, of which 2 were waited for; matrix products, arithmetic and copies ran while one was open for 1% of the time, Pallas kernels for 0%

profile of v2, /device:TPU:0, one launch (start us, length us, event | category | flops | bytes accessed | tf_op | source)
XLA Modules:
  0.0 257.7 jit_solution(10630083933610866006)
XLA Ops:
  7.2 0.0 copy-start.3
  7.2 0.0 copy-start.4
  7.2 0.0 all-gather.3.cloned.1.call-start
  7.2 0.7 fusion.10
  7.9 1.0 convert_element_type.16
  8.9 1.0 pad_maximum_fusion.2
  9.9 0.8 pad_maximum_fusion.1
  10.7 0.0 all-gather.3.cloned.1.call-update
  10.8 49.1 %all-gather.3.cloned.1.call-done = f32[4128,128]{1,0:T(8,128)} async-done(((f32[1032,128]{1,0:T(8,128)}), f32[4128,128]{1,0:T(8,128)}) %all-gather.3.cloned.1.call-update) | async-done | bytes 2113552 | tf_op jit(solution)/shard_map/all_gather | solution.py:360
  59.9 0.7 slice_bitcast_fusion
  60.6 0.1 convert_element_type.19
  60.7 0.0 copy-done.3
  60.7 0.0 copy-done.4
  60.7 0.2 select_reduce_fusion.3
  60.9 0.2 select_reduce_fusion.1
  61.2 0.1 broadcast_in_dim.100
  61.2 0.1 broadcast_in_dim.101
  61.3 0.1 broadcast_in_dim.96
  61.4 0.1 broadcast_in_dim.97
  61.5 0.1 compare_select_fusion
  61.6 0.1 reshape.408
  61.7 0.1 compare_select_fusion.1
  61.7 0.1 reshape.400
  61.8 2.3 gather_fusion.1
  64.1 0.1 broadcast_select_fusion
  64.2 1.3 collective-permute-start.1
  65.5 2.3 gather_fusion
  67.8 0.1 broadcast_select_fusion.1
  67.9 3.0 %collective-permute-start = (f32[160,128]{1,0:T(8,128)S(1)}, f32[160,128]{1,0:T(8,128)S(1)}, u32[]{:S(2)}, u32[]{:S(2)}) collective-permute-start(f32[160,128]{1,0:T(8,128)S(1)} %broadcast_select_fusion.1), channel_id=1, source_target_pairs={{0,4},{4,8},{8,12},{12,16},{16,20},{20,24},{24,28},{1,5},{5,9},{9,... | collective-permute-start | bytes 245768 | tf_op jit(solution)/shard_map/ppermute | solution.py:385
  70.9 0.0 collective-permute-done.1
  70.9 0.9 collective-permute-done
  71.8 1.7 pad_maximum_fusion.tiles_ref
  73.6 16.6 %shard_map.95 = (f32[2048,1152]{1,0:T(8,128)S(1)}, f32[2048,128]{1,0:T(8,128)S(1)}) custom-call(s32[2,144]{1,0:T(2,128)S(1)} %pad_add_fusion.offsets, f32[4448,128]{1,0:T(8,128)S(1)} %pad_maximum_fusion.tiles_ref), custom_call_target="tpu_custom_call" | custom-call | tf_op jit(solution)/shard_map/pallas_call | solution.py:73
  90.2 0.0 copy-start
  90.2 3.6 %copy-done = f32[2048,1152]{1,0:T(8,128)} copy-done((f32[2048,1152]{1,0:T(8,128)}, f32[2048,1152]{1,0:T(8,128)S(1)}, u32[]{:S(2)}) %copy-start) | copy-done | bytes 9437208
  93.8 0.0 copy-start.1
  93.8 1.0 copy-done.1
  94.8 152.7 %shard_map.96 = (f32[2048,128]{1,0:T(8,128)}, f32[2048,128]{1,0:T(8,128)}) custom-call(f32[2048,128]{1,0:T(8,128)} %prior_ref.1, s32[1,128]{1,0:T(1,128)} %bitcast.21, f32[2048,1152]{1,0:T(8,128)} %copy-done, f32[2048,128]{1,0:T(8,128)} %copy-done.1), custom_call_target="tpu_custom_call" | custom-call | tf_op jit(solution)/shard_map/pallas_call | solution.py:320
  247.5 0.0 copy-start.2
  247.5 2.4 copy.15
  249.9 0.0 copy-done.2
  249.9 1.0 copy.16
  (11 shorter events, 0.1 us)
Async XLA Ops:
  7.2 53.5 %copy-start.3 = (s32[10]{0:T(128)S(1)}, s32[10]{0:T(128)}, u32[]{:S(2)}) copy-start(s32[10]{0:T(128)} %constant.163) | copy-start | bytes 124
  7.2 53.5 %copy-start.4 = (s32[10]{0:T(128)S(1)}, s32[10]{0:T(128)}, u32[]{:S(2)}) copy-start(s32[10]{0:T(128)} %constant.160) | copy-start | bytes 124
  7.2 52.7 %all-gather.3.cloned.1.call-start = ((), (), s32[]{:S(2)}) async-start(), calls=%async_computation | async-start | bytes 2641920 | tf_op jit(solution)/shard_map/all_gather | solution.py:360
  64.2 6.7 %collective-permute-start.1 = (f32[160,128]{1,0:T(8,128)S(1)}, f32[160,128]{1,0:T(8,128)S(1)}, u32[]{:S(2)}, u32[]{:S(2)}) collective-permute-start(f32[160,128]{1,0:T(8,128)S(1)} %broadcast_select_fusion), channel_id=1, source_target_pairs={{4,0},{8,4},{12,8},{16,12},{20,16},{24,20},{28,24},{5,1},{9,5},{13... | collective-permute-start | bytes 245768 | tf_op jit(solution)/shard_map/ppermute | solution.py:386
  67.9 3.9 %collective-permute-start = (f32[160,128]{1,0:T(8,128)S(1)}, f32[160,128]{1,0:T(8,128)S(1)}, u32[]{:S(2)}, u32[]{:S(2)}) collective-permute-start(f32[160,128]{1,0:T(8,128)S(1)} %broadcast_select_fusion.1), channel_id=1, source_target_pairs={{0,4},{4,8},{8,12},{12,16},{16,20},{20,24},{24,28},{1,5},{5,9},{9,... | collective-permute-start | bytes 245768 | tf_op jit(solution)/shard_map/ppermute | solution.py:385
  90.2 3.6 %copy-start = (f32[2048,1152]{1,0:T(8,128)}, f32[2048,1152]{1,0:T(8,128)S(1)}, u32[]{:S(2)}) copy-start(f32[2048,1152]{1,0:T(8,128)S(1)} %get-tuple-element.16.band_ref) | copy-start | bytes 28311556
  93.8 1.0 copy-start.1
  247.5 2.4 copy-start.2
Sparse Core Ops, SparseCore 0:
  10.9 48.9 all-gather.2

commit v3 on v2

--- a/solution.py
+++ b/solution.py
@@ -31,7 +31,36 @@
     )
 
 
-def band_kernel(offsets, tiles_ref, band_ref, inv_ref):
+def split(value):
+    high = value.astype(jnp.bfloat16)
+    return high, (value - high.astype(jnp.float32)).astype(jnp.bfloat16)
+
+
+def dot16(left, right, dim):
+    return lax.dot_general(
+        left, right, (((dim,), (0,)), ((), ())), preferred_element_type=jnp.float32
+    )
+
+
+def mm_pair(left_high, left_low, right):
+    right_high, right_low = split(right)
+    wide = dot16(left_high, jnp.concatenate([right_high, right_low], axis=1), 1)
+    return wide[:, :TB] + (wide[:, TB:] + dot16(left_low, right_high, 1))
+
+
+def mm_split(left, right):
+    return mm_pair(*split(left), right)
+
+
+def mm_t_split(left, right):
+    left_high, left_low = split(left)
+    right_high, right_low = split(right)
+    return dot16(left_high, right_high, 0) + (
+        dot16(left_high, right_low, 0) + dot16(left_low, right_high, 0)
+    )
+
+
+def band_kernel(offsets, tiles_ref, high_ref, low_ref, inv_ref, band_ref):
     row = pl.program_id(0)
     places = lax.broadcasted_iota(jnp.int32, (TB, TB), 0).astype(jnp.float32)
 
@@ -61,6 +90,7 @@
         def _():
             band_ref[:, lanes] += transposed_tile(backward)
 
+    high_ref[...], low_ref[...] = split(band_ref[...])
     folded = band_ref[:, 0:TB]
     for o in range(1, SPAN):
         folded = folded + band_ref[:, o * TB : (o + 1) * TB]
@@ -78,11 +108,14 @@
             in_specs=[pl.BlockSpec(tiles.shape, lambda i, _: (0, 0))],
             out_specs=[
                 pl.BlockSpec((TB, SPAN * TB), lambda i, _: (i, 0)),
+                pl.BlockSpec((TB, SPAN * TB), lambda i, _: (i, 0)),
                 pl.BlockSpec((TB, TB), lambda i, _: (i, 0)),
             ],
+            scratch_shapes=[pltpu.VMEM((TB, SPAN * TB), jnp.float32)],
         ),
         out_shape=[
-            jax.ShapeDtypeStruct((row_blocks * TB, SPAN * TB), jnp.float32),
+            jax.ShapeDtypeStruct((row_blocks * TB, SPAN * TB), jnp.bfloat16),
+            jax.ShapeDtypeStruct((row_blocks * TB, SPAN * TB), jnp.bfloat16),
             jax.ShapeDtypeStruct((row_blocks * TB, TB), jnp.float32),
         ],
         compiler_params=pltpu.CompilerParams(vmem_limit_bytes=32 * 1024 * 1024),
@@ -127,7 +160,7 @@
 
 
 def cg_kernel(
-    nodes, cols, prior_ref, queries_ref, band_ref, inv_ref, x_ref, r_ref,
+    nodes, cols, prior_ref, queries_ref, high_ref, low_ref, inv_ref, x_ref, r_ref,
     vext, direc, image, wbuf, acc, spread, column_sums, total, gram_inv, curv_inv, curv_old,
     ratio_ref, step_ref, halo_send, halo_recv, spread_send, spread_recv, col_send, col_recv,
     back_send, back_recv,
@@ -194,7 +227,9 @@
     def iteration(it, carry):
         def apply_block(b, inner):
             at = pl.multiple_of(b * TB, TB)
-            product = mm(band_ref[pl.ds(at, TB), :], vext[it, pl.ds(at, SPAN * TB), :])
+            product = mm_pair(
+                high_ref[pl.ds(at, TB), :], low_ref[pl.ds(at, TB), :], vext[it, pl.ds(at, SPAN * TB), :]
+            )
             mine = pl.ds(at, TB)
             wbuf[mine, :] = r_ref[mine, :] - ALPHA * inv_ref[mine, :] * product
             return inner
@@ -216,7 +251,7 @@
         def add_gram(c, inner):
             at = pl.ds(pl.multiple_of(c * chunk, chunk), chunk)
             part = r_ref[at, :]
-            both = mm_t(part, jnp.concatenate([part, wbuf[at, :]], axis=1))
+            both = mm_t_split(part, jnp.concatenate([part, wbuf[at, :]], axis=1))
             acc[0:TB, :] += both[:, 0:TB]
             acc[TB : 2 * TB, :] += both[:, TB : 2 * TB]
             return inner
@@ -284,12 +319,12 @@
         def update_rows(c, inner):
             start = pl.multiple_of(c * chunk, chunk)
             at = pl.ds(start, chunk)
-            fresh = r_ref[at, :] + mm(direc[at, :], ratio_ref[...])
+            fresh = r_ref[at, :] + mm_split(direc[at, :], ratio_ref[...])
             direc[at, :] = fresh
-            x_ref[at, :] += mm(fresh, step_ref[...])
-            turned = wbuf[at, :] + mm(image[at, :], ratio_ref[...])
+            x_ref[at, :] += mm_split(fresh, step_ref[...])
+            turned = wbuf[at, :] + mm_split(image[at, :], ratio_ref[...])
             image[at, :] = turned
-            left_over = r_ref[at, :] - mm(turned, step_ref[...])
+            left_over = r_ref[at, :] - mm_split(turned, step_ref[...])
             r_ref[at, :] = left_over
             vext[it + 1, pl.ds(HALO + start, chunk), :] = inv_ref[at, :] * left_over
             return inner
@@ -309,7 +344,7 @@
     lax.fori_loop(0, ITERS, iteration, 0)
 
 
-def run_cg(nodes, cols, prior, queries, band, inv):
+def run_cg(nodes, cols, prior, queries, high, low, inv):
     rows = prior.shape[0]
     share = 2 * TB // nodes
     full = pl.BlockSpec(memory_space=pltpu.VMEM)
@@ -319,7 +354,7 @@
     tall = pltpu.VMEM((2 * TB, TB), jnp.float32)
     return pl.pallas_call(
         functools.partial(cg_kernel, nodes, cols),
-        in_specs=[full] * 4,
+        in_specs=[full] * 5,
         out_specs=[full] * 2,
         out_shape=[shape, shape],
         scratch_shapes=[
@@ -336,7 +371,7 @@
         compiler_params=pltpu.CompilerParams(
             collective_id=0, has_side_effects=True, vmem_limit_bytes=56 * 1024 * 1024
         ),
-    )(prior, queries, band, inv)
+    )(prior, queries, high, low, inv)
 
 
 def body(prior, queries, tile_rows, tile_cols, tile_ids, tile_weights):
@@ -398,8 +433,8 @@
     c_next = i_at - (blocks - BAND)
     next_at = edge_at + (EDGE + c_next * (c_next + 1) // 2 + back_row - blocks) * 2 * KT
     backward = jnp.where(back_row < 0, prev_at, jnp.where(back_row >= blocks, next_at, inside))
-    band, inv = build_band(jnp.stack([forward, backward]), tiles, row_blocks)
-    return tuple(run_cg(nodes, cols, prior, queries[None, :], band, inv))
+    high, low, inv = build_band(jnp.stack([forward, backward]), tiles, row_blocks)
+    return tuple(run_cg(nodes, cols, prior, queries[None, :], high, low, inv))
 
 
 def solution(mesh):

time: 258 us -> 241 us (0.934)
  Pallas kernels: 169 us -> 151 us
    pallas_call x1, Pallas kernels: 153 us -> 134 us  [run_cg(): pl.pallas_call(functools.partial(cg_kernel, nodes, cols), in_specs=[full]...]
    unnamed x14 -> x16, local copies, waits for them, and re-layouts: 8.64 us -> 9.32 us
where the time goes in v3:
time: 241 us; the launch traced here: 240 us
  Pallas kernels  151 us (63%)
  waiting for transfers between devices  50 us (21%)
  local copies, waits for them, and re-layouts  14.4 us (6%)
  between operations  14.2 us (6%)
  other arithmetic  6.04 us (3%)
  starting transfers between devices  4.37 us (2%)
    pallas_call x1, Pallas kernels, run_cg(): pl.pallas_call(functools.partial(cg_kernel, nodes, cols), in_specs=[full]...  134 us
    all_gather x1, waiting for transfers between devices, body(): gathered = lax.all_gather(flat, 'cols', axis=0, tiled=False)  49.1 us
    pallas_call x1, Pallas kernels, build_band(): pl.pallas_call(band_kernel, grid_spec=pltpu.PrefetchScalarGridSpec(num_sc...  17.6 us
    unnamed x16, local copies, waits for them, and re-layouts  9.32 us
  transfers between devices with their start and end apart: 3, of which 2 were waited for; matrix products, arithmetic and copies ran while one was open for 1% of the time, Pallas kernels for 0%

profile of v3, /device:TPU:0, one launch (start us, length us, event | category | flops | bytes accessed | tf_op | source)
XLA Modules:
  0.0 240.4 jit_solution(1408737335188002090)
XLA Ops:
  7.2 0.0 copy-start.4
  7.2 0.0 copy-start.5
  7.2 0.0 all-gather.3.cloned.1.call-start
  7.2 0.7 fusion.10
  7.9 1.0 convert_element_type.16
  8.9 1.0 pad_maximum_fusion.2
  9.9 0.8 pad_maximum_fusion.1
  10.7 0.0 all-gather.3.cloned.1.call-update
  10.8 49.1 %all-gather.3.cloned.1.call-done = f32[4128,128]{1,0:T(8,128)} async-done(((f32[1032,128]{1,0:T(8,128)}), f32[4128,128]{1,0:T(8,128)}) %all-gather.3.cloned.1.call-update) | async-done | bytes 2113552 | tf_op jit(solution)/shard_map/all_gather | solution.py:395
  59.9 0.7 slice_bitcast_fusion
  60.6 0.1 convert_element_type.19
  60.7 0.0 copy-done.4
  60.7 0.0 copy-done.5
  60.7 0.2 select_reduce_fusion.3
  60.9 0.2 select_reduce_fusion.1
  61.2 0.1 broadcast_in_dim.100
  61.2 0.1 broadcast_in_dim.101
  61.3 0.1 broadcast_in_dim.96
  61.4 0.1 broadcast_in_dim.97
  61.5 0.1 compare_select_fusion
  61.6 0.1 reshape.408
  61.7 0.1 compare_select_fusion.1
  61.7 0.1 reshape.400
  61.8 2.3 gather_fusion.1
  64.1 0.1 broadcast_select_fusion
  64.2 1.3 collective-permute-start.1
  65.5 2.3 gather_fusion
  67.8 0.1 broadcast_select_fusion.1
  67.9 3.0 %collective-permute-start = (f32[160,128]{1,0:T(8,128)S(1)}, f32[160,128]{1,0:T(8,128)S(1)}, u32[]{:S(2)}, u32[]{:S(2)}) collective-permute-start(f32[160,128]{1,0:T(8,128)S(1)} %broadcast_select_fusion.1), channel_id=1, source_target_pairs={{0,4},{4,8},{8,12},{12,16},{16,20},{20,24},{24,28},{1,5},{5,9},{9,... | collective-permute-start | bytes 245768 | tf_op jit(solution)/shard_map/ppermute | solution.py:420
  70.9 0.0 collective-permute-done.1
  70.9 0.9 collective-permute-done
  71.8 1.7 pad_maximum_fusion.tiles_ref
  73.6 17.6 %shard_map.95 = (bf16[2048,1152]{1,0:T(8,128)(2,1)S(1)}, bf16[2048,1152]{1,0:T(8,128)(2,1)S(1)}, f32[2048,128]{1,0:T(8,128)S(1)}) custom-call(s32[2,144]{1,0:T(2,128)S(1)} %pad_add_fusion.offsets, f32[4448,128]{1,0:T(8,128)S(1)} %pad_maximum_fusion.tiles_ref), custom_call_target="tpu_custom_call" | custom-call | tf_op jit(solution)/shard_map/pallas_call | solution.py:103
  91.2 0.0 copy-start
  91.2 2.1 copy-done
  93.3 0.0 copy-start.1
  93.3 2.2 copy-done.1
  95.5 0.0 copy-start.2
  95.5 1.0 copy-done.2
  96.4 133.8 %shard_map.96 = (f32[2048,128]{1,0:T(8,128)}, f32[2048,128]{1,0:T(8,128)}) custom-call(f32[2048,128]{1,0:T(8,128)} %prior_ref.1, s32[1,128]{1,0:T(1,128)} %bitcast.21, bf16[2048,1152]{1,0:T(8,128)(2,1)} %copy-done, bf16[2048,1152]{1,0:T(8,128)(2,1)} %copy-done.1, f32[2048,128]{1,0:T(8,128)} %copy-done.2), custom_call_target="tpu_custom_call" | custom-call | tf_op jit(solution)/shard_map/pallas_call | solution.py:355
  230.2 0.0 copy-start.3
  230.2 2.4 copy.15
  232.6 0.0 copy-done.3
  232.6 1.0 copy.16
  (11 shorter events, 0.1 us)
Async XLA Ops:
  7.2 53.5 %copy-start.4 = (s32[10]{0:T(128)S(1)}, s32[10]{0:T(128)}, u32[]{:S(2)}) copy-start(s32[10]{0:T(128)} %constant.163) | copy-start | bytes 124
  7.2 53.5 %copy-start.5 = (s32[10]{0:T(128)S(1)}, s32[10]{0:T(128)}, u32[]{:S(2)}) copy-start(s32[10]{0:T(128)} %constant.160) | copy-start | bytes 124
  7.2 52.7 %all-gather.3.cloned.1.call-start = ((), (), s32[]{:S(2)}) async-start(), calls=%async_computation | async-start | bytes 2641920 | tf_op jit(solution)/shard_map/all_gather | solution.py:395
  64.2 6.7 %collective-permute-start.1 = (f32[160,128]{1,0:T(8,128)S(1)}, f32[160,128]{1,0:T(8,128)S(1)}, u32[]{:S(2)}, u32[]{:S(2)}) collective-permute-start(f32[160,128]{1,0:T(8,128)S(1)} %broadcast_select_fusion), channel_id=1, source_target_pairs={{4,0},{8,4},{12,8},{16,12},{20,16},{24,20},{28,24},{5,1},{9,5},{13... | collective-permute-start | bytes 245768 | tf_op jit(solution)/shard_map/ppermute | solution.py:421
  67.9 3.9 %collective-permute-start = (f32[160,128]{1,0:T(8,128)S(1)}, f32[160,128]{1,0:T(8,128)S(1)}, u32[]{:S(2)}, u32[]{:S(2)}) collective-permute-start(f32[160,128]{1,0:T(8,128)S(1)} %broadcast_select_fusion.1), channel_id=1, source_target_pairs={{0,4},{4,8},{8,12},{12,16},{16,20},{20,24},{24,28},{1,5},{5,9},{9,... | collective-permute-start | bytes 245768 | tf_op jit(solution)/shard_map/ppermute | solution.py:420
  91.2 2.1 copy-start
  93.3 2.2 copy-start.1
  95.5 1.0 copy-start.2
  230.2 2.4 copy-start.3
Sparse Core Ops, SparseCore 0:
  10.9 48.9 all-gather.2

commit v4 on v3

--- a/solution.py
+++ b/solution.py
@@ -374,6 +374,72 @@
     )(prior, queries, high, low, inv)
 
 
+def gather_kernel(cols, parts, shard_ref, out_ref, send_sem, recv_sem):
+    node = lax.axis_index("nodes")
+    col = lax.axis_index("cols")
+    piece = shard_ref.shape[0] // parts
+    barrier = pltpu.get_barrier_semaphore()
+    for step in (1, cols - 1):
+        pl.semaphore_signal(
+            barrier, inc=1, device_id=(node, (col + step) % cols), device_id_type=MESH
+        )
+    out_ref[col] = shard_ref[...]
+    pl.semaphore_wait(barrier, 2)
+
+    def hop(way, h, p, source):
+        at = pl.ds(p * piece, piece)
+        target = (col + 1) % cols if way == 0 else (col + cols - 1) % cols
+        return pltpu.make_async_remote_copy(
+            src_ref=out_ref.at[source, at, :], dst_ref=out_ref.at[source, at, :],
+            send_sem=send_sem.at[way, h, p], recv_sem=recv_sem.at[way, h, p],
+            device_id=(node, target), device_id_type=MESH,
+        )
+
+    for h in range(cols):
+        for p in range(parts):
+            for way in range(2):
+                source = col - h if way == 0 else col + h
+                held = source >= 0 if way == 0 else source < cols
+                onward = col < cols - 1 if way == 0 else col > 0
+                if h > 0:
+
+                    @pl.when(held)
+                    def _():
+                        hop(way, h - 1, p, source).wait_recv()
+
+                if h < cols - 1:
+
+                    @pl.when(held & onward)
+                    def _():
+                        hop(way, h, p, source).start()
+
+    for h in range(cols - 1):
+        for p in range(parts):
+            for way in range(2):
+                source = col - h if way == 0 else col + h
+                held = source >= 0 if way == 0 else source < cols
+                onward = col < cols - 1 if way == 0 else col > 0
+
+                @pl.when(held & onward)
+                def _():
+                    hop(way, h, p, source).wait_send()
+
+
+def gather_cols(cols, flat):
+    parts = 3 if flat.shape[0] % 24 == 0 else 1
+    full = pl.BlockSpec(memory_space=pltpu.VMEM)
+    return pl.pallas_call(
+        functools.partial(gather_kernel, cols, parts),
+        in_specs=[full],
+        out_specs=full,
+        out_shape=jax.ShapeDtypeStruct((cols,) + flat.shape, flat.dtype),
+        scratch_shapes=[pltpu.SemaphoreType.DMA((2, cols, parts))] * 2,
+        compiler_params=pltpu.CompilerParams(
+            collective_id=1, has_side_effects=True, vmem_limit_bytes=32 * 1024 * 1024
+        ),
+    )(flat)
+
+
 def body(prior, queries, tile_rows, tile_cols, tile_ids, tile_weights):
     rows_dev = prior.shape[0]
     nodes = lax.axis_size("nodes")
@@ -392,7 +458,7 @@
     meta_rows = 8 * (-(-per_dev // (8 * TB)))
     meta = jnp.full((meta_rows * TB,), -1.0, jnp.float32).at[:per_dev].set(keys)
     flat = jnp.concatenate([packed.reshape(per_dev * 2 * KT, TB), meta.reshape(meta_rows, TB)])
-    gathered = lax.all_gather(flat, "cols", axis=0, tiled=False)
+    gathered = gather_cols(cols, flat)
     stride = flat.shape[0]
     slot_keys = gathered[:, per_dev * 2 * KT :, :].reshape(cols, -1)[:, :per_dev].reshape(-1).astype(jnp.int32)
     slot = jnp.arange(cols * per_dev, dtype=jnp.int32)

time: 241 us -> 212 us (0.88)
  waiting for transfers between devices: 50 us -> 0.59 us
  Pallas kernels: 151 us -> 192 us
  between operations: 14.2 us -> 0.84 us
  local copies, waits for them, and re-layouts: 14.4 us -> 10.5 us
    all_gather x1 -> x0, waiting for transfers between devices: 49.1 us -> none  [body(): gathered = lax.all_gather(flat, 'cols', axis=0, tiled=False)]
    pallas_call x0 -> x1, Pallas kernels: none -> 39.5 us  [gather_cols(): pl.pallas_call(functools.partial(gather_kernel, cols, parts), in_specs=[f...]
    gather x2, local copies, waits for them, and re-layouts: 4.53 us -> 1.36 us  [pick(): chosen = group_tiles[found]]
    pallas_call x1, Pallas kernels: 134 us -> 137 us  [run_cg(): pl.pallas_call(functools.partial(cg_kernel, nodes, cols), in_specs=[full]...]
  transfers between devices with their start and end apart: 3 -> 2, of which waited for: 2 -> 1; matrix products, arithmetic and copies ran while one was open for 1% -> 1% of each run, Pallas kernels for 0% -> 0%
where the time goes in v4:
time: 212 us
  Pallas kernels  192 us (91%)
  local copies, waits for them, and re-layouts  10.5 us (5%)
  starting transfers between devices  4.33 us (2%)
  other arithmetic  3.66 us (2%)
    pallas_call x1, Pallas kernels, run_cg(): pl.pallas_call(functools.partial(cg_kernel, nodes, cols), in_specs=[full]...  137 us
    pallas_call x1, Pallas kernels, gather_cols(): pl.pallas_call(functools.partial(gather_kernel, cols, parts), in_specs=[f...  39.5 us
    pallas_call x1, Pallas kernels, build_band(): pl.pallas_call(band_kernel, grid_spec=pltpu.PrefetchScalarGridSpec(num_sc...  15.5 us
    unnamed x16, local copies, waits for them, and re-layouts  8.6 us
  transfers between devices with their start and end apart: 2, of which 1 were waited for; matrix products, arithmetic and copies ran while one was open for 1% of the time, Pallas kernels for 0%

profile of v4, /device:TPU:0, one launch (start us, length us, event | category | flops | bytes accessed | tf_op | source)
XLA Modules:
  0.0 211.7 jit_solution(11893569179942927345)
XLA Ops:
  0.6 0.7 fusion.10
  1.3 1.0 convert_element_type.16
  2.3 0.0 copy-start.4
  2.3 0.0 copy-start.5
  2.3 1.0 pad_maximum_fusion.2
  3.4 39.5 %shard_map.95 = f32[4,1032,128]{2,1,0:T(8,128)S(1)} custom-call(f32[1032,128]{1,0:T(8,128)S(1)} %pad_maximum_fusion.1.shard_ref), custom_call_target="tpu_custom_call" | custom-call | tf_op jit(solution)/shard_map/pallas_call | solution.py:431
  42.9 0.1 convert_element_type.19
  43.0 0.0 copy-done.4
  43.0 0.0 copy-done.5
  43.0 0.2 select_reduce_fusion.3
  43.2 0.1 broadcast_in_dim.100
  43.2 0.1 broadcast_in_dim.101
  43.3 0.1 compare_select_fusion
  43.4 0.1 reshape.408
  43.5 0.7 gather_fusion.1
  44.2 0.1 broadcast_select_fusion
  44.3 1.3 collective-permute-start.1
  45.6 0.1 broadcast_in_dim.96
  45.7 0.1 broadcast_in_dim.97
  45.7 0.1 compare_select_fusion.1
  45.8 0.1 reshape.400
  45.9 0.7 gather_fusion
  46.6 0.1 broadcast_select_fusion.1
  46.7 3.0 %collective-permute-start = (f32[160,128]{1,0:T(8,128)S(1)}, f32[160,128]{1,0:T(8,128)S(1)}, u32[]{:S(2)}, u32[]{:S(2)}) collective-permute-start(f32[160,128]{1,0:T(8,128)S(1)} %broadcast_select_fusion.1), channel_id=1, source_target_pairs={{0,4},{4,8},{8,12},{12,16},{16,20},{20,24},{24,28},{1,5},{5,9},{9,... | collective-permute-start | bytes 245768 | tf_op jit(solution)/shard_map/ppermute | solution.py:486
  49.8 0.2 select_reduce_fusion.1
  50.0 0.0 collective-permute-done.1
  50.0 0.6 collective-permute-done
  50.6 0.1 pad_maximum_fusion.tiles_ref
  50.8 15.5 %shard_map.96 = (bf16[2048,1152]{1,0:T(8,128)(2,1)S(1)}, bf16[2048,1152]{1,0:T(8,128)(2,1)S(1)}, f32[2048,128]{1,0:T(8,128)S(1)}) custom-call(s32[2,144]{1,0:T(2,128)S(1)} %pad_add_fusion.offsets, f32[4448,128]{1,0:T(8,128)S(1)} %pad_maximum_fusion.tiles_ref), custom_call_target="tpu_custom_call" | custom-call | tf_op jit(solution)/shard_map/pallas_call | solution.py:103
  66.3 0.0 copy-start
  66.3 2.1 copy-done
  68.4 0.0 copy-start.1
  68.4 2.2 %copy-done.1 = bf16[2048,1152]{1,0:T(8,128)(2,1)} copy-done((bf16[2048,1152]{1,0:T(8,128)(2,1)}, bf16[2048,1152]{1,0:T(8,128)(2,1)S(1)}, u32[]{:S(2)}) %copy-start.1) | copy-done | bytes 4718616
  70.6 0.0 copy-start.2
  70.6 1.0 copy-done.2
  71.6 136.8 %shard_map.97 = (f32[2048,128]{1,0:T(8,128)}, f32[2048,128]{1,0:T(8,128)}) custom-call(f32[2048,128]{1,0:T(8,128)} %prior_ref.1, s32[1,128]{1,0:T(1,128)} %bitcast.23, bf16[2048,1152]{1,0:T(8,128)(2,1)} %copy-done, bf16[2048,1152]{1,0:T(8,128)(2,1)} %copy-done.1, f32[2048,128]{1,0:T(8,128)} %copy-done.2), custom_call_target="tpu_custom_call" | custom-call | tf_op jit(solution)/shard_map/pallas_call | solution.py:355
  208.4 0.0 copy-start.3
  208.4 2.4 %copy.15 = f32[2048,128]{1,0:T(8,128)} copy(f32[2048,128]{1,0:T(8,128)} %get-tuple-element.32) | data formatting | bytes 2097152
  210.7 0.0 copy-done.3
  210.7 1.0 copy.16
  (13 shorter events, 0.1 us)
Async XLA Ops:
  2.3 40.6 %copy-start.4 = (s32[10]{0:T(128)S(1)}, s32[10]{0:T(128)}, u32[]{:S(2)}) copy-start(s32[10]{0:T(128)} %constant.163) | copy-start | bytes 124
  2.3 40.6 %copy-start.5 = (s32[10]{0:T(128)S(1)}, s32[10]{0:T(128)}, u32[]{:S(2)}) copy-start(s32[10]{0:T(128)} %constant.160) | copy-start | bytes 124
  44.3 5.8 %collective-permute-start.1 = (f32[160,128]{1,0:T(8,128)S(1)}, f32[160,128]{1,0:T(8,128)S(1)}, u32[]{:S(2)}, u32[]{:S(2)}) collective-permute-start(f32[160,128]{1,0:T(8,128)S(1)} %broadcast_select_fusion), channel_id=1, source_target_pairs={{4,0},{8,4},{12,8},{16,12},{20,16},{24,20},{28,24},{5,1},{9,5},{13... | collective-permute-start | bytes 245768 | tf_op jit(solution)/shard_map/ppermute | solution.py:487
  46.7 3.9 %collective-permute-start = (f32[160,128]{1,0:T(8,128)S(1)}, f32[160,128]{1,0:T(8,128)S(1)}, u32[]{:S(2)}, u32[]{:S(2)}) collective-permute-start(f32[160,128]{1,0:T(8,128)S(1)} %broadcast_select_fusion.1), channel_id=1, source_target_pairs={{0,4},{4,8},{8,12},{12,16},{16,20},{20,24},{24,28},{1,5},{5,9},{9,... | collective-permute-start | bytes 245768 | tf_op jit(solution)/shard_map/ppermute | solution.py:486
  66.3 2.1 %copy-start = (bf16[2048,1152]{1,0:T(8,128)(2,1)}, bf16[2048,1152]{1,0:T(8,128)(2,1)S(1)}, u32[]{:S(2)}) copy-start(bf16[2048,1152]{1,0:T(8,128)(2,1)S(1)} %get-tuple-element.17.high_ref) | copy-start | bytes 14155780
  68.4 2.2 %copy-start.1 = (bf16[2048,1152]{1,0:T(8,128)(2,1)}, bf16[2048,1152]{1,0:T(8,128)(2,1)S(1)}, u32[]{:S(2)}) copy-start(bf16[2048,1152]{1,0:T(8,128)(2,1)S(1)} %get-tuple-element.18.low_ref) | copy-start | bytes 14155780
  70.6 1.0 copy-start.2
  208.4 2.4 %copy-start.3 = (f32[2048,128]{1,0:T(8,128)S(1)}, f32[2048,128]{1,0:T(8,128)}, u32[]{:S(2)}) copy-start(f32[2048,128]{1,0:T(8,128)} %get-tuple-element.33) | copy-start | bytes 3145732
